TPU v7x, 128 devices: a whole 4x4x4 slice. The times are simulated.
128 devices in a mesh: section: 16 (over z_lo, y, core), tensor: 8 (over z_hi, x).
Axes of the slice: x: 4, y: 4, z: 4 (z_hi: 2, z_lo: 2; z = z_hi * 2 + z_lo), core: 2. Of those that a mesh axis runs over, the one named last changes fastest.
Arguments:
- inputs_down: bfloat16 [16, 2, 240, 2048], P('section', None, 'tensor'), may hold values from -6 to 6
- inputs_up: bfloat16 [16, 2, 240, 2048], P('section', None, 'tensor'), may hold values from -6 to 6
- grads_down: bfloat16 [16, 240, 2048], P('section', 'tensor'), may hold values from -6 to 6
- grads_up: bfloat16 [16, 240, 2048], P('section', 'tensor'), may hold values from -6 to 6
- loss_grads: bfloat16 [2, 240, 2048], P(None, 'tensor'), may hold values from -6 to 6
- first_down: bfloat16 [16, 2048, 4096], P('section', None, 'tensor'), may hold values from -6 to 6
- second_down: bfloat16 [16, 4096, 2048], P('section', 'tensor'), may hold values from -6 to 6
- first_up: bfloat16 [16, 2048, 4096], P('section', None, 'tensor'), may hold values from -6 to 6
- second_up: bfloat16 [16, 4096, 2048], P('section', 'tensor'), may hold values from -6 to 6
- momentum_first: bfloat16 [16, 2048, 4096], P('section', None, 'tensor'), may hold values from -3 to 3
- momentum_second: bfloat16 [16, 4096, 2048], P('section', 'tensor'), may hold values from -3 to 3
Outputs:
- first_new: bfloat16 [16, 2048, 4096], P('section', None, 'tensor')
- second_new: bfloat16 [16, 4096, 2048], P('section', 'tensor')
- momentum_one: bfloat16 [16, 2048, 4096], P('section', None, 'tensor')
- momentum_two: bfloat16 [16, 4096, 2048], P('section', 'tensor')
- passed_down: bfloat16 [16, 240, 2048], P('section', 'tensor')
- passed_up: bfloat16 [16, 240, 2048], P('section', 'tensor')
All inputs are finite; a program needn't handle non-finite values.
Results may differ from a plain program's by a relative error of at most 0.0063.
Values may be sent and summed in bfloat16 or wider, within the bound.
A program may use at most 128 MiB of HBM per device.

v0:
```python
import jax
import jax.numpy as jnp
from jax import lax
from jax.sharding import PartitionSpec as P

D = 2048
FF = 4096


epsilon = 1e-05
learning_rate = 0.25
momentum_decay = 0.9
tanh_scale = 0.7978845608028654
cubic_term = 0.044715


def passed_along(value, axis, by):
    devices = lax.axis_size(axis)
    pairs = [(i, i + by) for i in range(devices) if 0 <= i + by < devices]
    return lax.ppermute(value, axis, pairs)


def partner(value, axis, bit):
    mask = 2**bit
    pairs = [(source, source ^ mask) for source in range(lax.axis_size(axis))]
    return lax.ppermute(value, axis, pairs)


def gelu_with_slope(preact):
    tanh_input = tanh_scale * (preact + cubic_term * preact * preact * preact)
    tangent = jnp.tanh(tanh_input)
    values = 0.5 * preact * (1.0 + tangent)
    slopes = 0.5 * (1.0 + tangent) + 0.5 * preact * (1.0 - tangent * tangent) * tanh_scale * (
        1.0 + 3.0 * cubic_term * preact * preact
    )
    return (values, slopes)


def normalize(inputs):
    widened = inputs.astype(jnp.float32)
    centred = widened - jnp.mean(widened, axis=-1, keepdims=True)
    inverse_scale = lax.rsqrt(jnp.mean(centred * centred, axis=-1, keepdims=True) + epsilon)
    return (centred * inverse_scale, inverse_scale)


def contract_rows(left_side, right_side):
    return lax.dot_general(
        left_side, right_side, (((0,), (0,)), ((), ())), preferred_element_type=jnp.float32
    )


def contract_last(left_side, right_side):
    return lax.dot_general(
        left_side, right_side, (((1,), (1,)), ((), ())), preferred_element_type=jnp.float32
    )


def body(
    inputs_down,
    inputs_up,
    grads_down,
    grads_up,
    loss_grads,
    first_down,
    second_down,
    first_up,
    second_up,
    momentum_first,
    momentum_second,
):
    section_count = lax.axis_size("section")
    position = lax.axis_index("section")
    row_count = grads_down.shape[1]
    row_start = lax.axis_index("tensor") * row_count
    model_width = first_down.shape[1]
    hidden_local = first_down.shape[2]
    firsts = (first_down[0], first_up[0])
    seconds = (second_down[0], second_up[0])
    cotans = (grads_down[0], grads_up[0])
    kept_cotans = []
    records = []
    passed = []
    for step_index in range(2):
        gathered = (
            lax.all_gather(inputs_down[0, step_index], "tensor", axis=0, tiled=True),
            lax.all_gather(inputs_up[0, step_index], "tensor", axis=0, tiled=True),
            lax.all_gather(cotans[0], "tensor", axis=0, tiled=True),
            lax.all_gather(cotans[1], "tensor", axis=0, tiled=True),
        )
        results = []
        for branch in range(2):
            normed, inverse_scale = normalize(gathered[branch])
            normed_low = normed.astype(jnp.bfloat16)
            preact = jnp.dot(
                normed_low, firsts[branch], preferred_element_type=jnp.float32
            ) * D ** (-0.5)
            values, slopes = gelu_with_slope(preact)
            activation = values.astype(jnp.bfloat16)
            grad_activation = contract_last(gathered[2 + branch], seconds[branch]) * FF ** (-0.5)
            grad_preact = (grad_activation * slopes).astype(jnp.bfloat16)
            results.append(
                (normed, inverse_scale, normed_low, activation, grad_preact, gathered[2 + branch])
            )
        pieces = []
        for hidden_branch in range(2):
            row_piece = results[hidden_branch][4]
            pieces.append(contract_last(row_piece, firsts[hidden_branch]) * D ** (-0.5))
        grad_normed_both = lax.psum_scatter(
            jnp.concatenate(pieces, axis=1), "tensor", scatter_dimension=0, tiled=True
        )
        passed = []
        for branch in range(2):
            own_normed = lax.dynamic_slice_in_dim(results[branch][0], row_start, row_count, 0)
            own_scale = lax.dynamic_slice_in_dim(results[branch][1], row_start, row_count, 0)
            grad_normed = grad_normed_both[:, branch * model_width : (branch + 1) * model_width]
            first_mean = jnp.mean(grad_normed, axis=-1, keepdims=True)
            second_mean = jnp.mean(grad_normed * own_normed, axis=-1, keepdims=True)
            grad_inputs = cotans[branch].astype(jnp.float32) + own_scale * (
                grad_normed - first_mean - own_normed * second_mean
            )
            passed.append(grad_inputs.astype(jnp.bfloat16))
        records.append(results)
        kept_cotans.append(cotans)
        if step_index == 0:
            from_above = passed_along(passed[0], "section", -1)
            from_below = passed_along(passed[1], "section", 1)
            cotans = (
                jnp.where(position == section_count - 1, loss_grads[0], from_above),
                jnp.where(position == 0, loss_grads[1], from_below),
            )

    def joined(branch, item):
        return jnp.concatenate([records[0][branch][item], records[1][branch][item]], axis=0)

    down_first = contract_rows(joined(0, 2), joined(0, 4)) * D ** (-0.5)
    down_second = contract_rows(joined(0, 3), joined(0, 5)) * FF ** (-0.5)
    bit_total = section_count.bit_length() - 1
    up_first = contract_rows(joined(1, 2), joined(1, 4)) * D ** (-0.5)
    up_second = contract_rows(joined(1, 3), joined(1, 5)) * FF ** (-0.5)
    payload = jnp.concatenate(
        [up_first.astype(jnp.bfloat16).reshape(-1), up_second.astype(jnp.bfloat16).reshape(-1)]
    )
    for bit_index in range(bit_total):
        payload = partner(payload, "section", bit_index)
    size_one = model_width * hidden_local
    mirror_first = payload[:size_one].reshape(model_width, hidden_local)
    mirror_second = payload[size_one:].reshape(hidden_local, model_width)
    total_first = down_first + mirror_first.astype(jnp.float32)
    total_second = down_second + mirror_second.astype(jnp.float32)
    moment_first = momentum_decay * momentum_first[0].astype(jnp.float32) + total_first
    moment_second = momentum_decay * momentum_second[0].astype(jnp.float32) + total_second
    first_new = (first_down[0].astype(jnp.float32) - learning_rate * moment_first).astype(
        jnp.bfloat16
    )
    second_new = (second_down[0].astype(jnp.float32) - learning_rate * moment_second).astype(
        jnp.bfloat16
    )
    return (
        first_new[None],
        second_new[None],
        moment_first.astype(jnp.bfloat16)[None],
        moment_second.astype(jnp.bfloat16)[None],
        passed[0][None],
        passed[1][None],
    )


def solution(mesh):
    placed = (
        P("section", None, "tensor", None),
        P("section", None, "tensor", None),
        P("section", "tensor", None),
        P("section", "tensor", None),
        P(None, "tensor", None),
        P("section", None, "tensor"),
        P("section", "tensor", None),
        P("section", None, "tensor"),
        P("section", "tensor", None),
        P("section", None, "tensor"),
        P("section", "tensor", None),
    )
    return jax.shard_map(
        body,
        mesh=mesh,
        in_specs=placed,
        out_specs=(
            P("section", None, "tensor"),
            P("section", "tensor", None),
            P("section", None, "tensor"),
            P("section", "tensor", None),
            P("section", "tensor", None),
            P("section", "tensor", None),
        ),
        check_vma=False,
    )
```

profile of v0, /device:TPU:0, one launch (start us, length us, event | category | flops | bytes accessed | tf_op | source)
XLA Modules:
  0.0 823.3 jit_solution(11953718026809434699)
XLA Ops:
  7.2 1.6 fusion.134
  8.9 39.5 %all-gather.4 = bf16[1,1,240,2048]{3,1,0,2:T(2,128)(2,1)S(1)} all-gather(bf16[1,1,30,2048]{3,1,0,2:T(2,128)(2,1)S(1)} %get-tuple-element.37), channel_id=6, replica_groups=mesh['section'=16,'tensor'=8] {'tensor'}, dimensions={2}, use_global_device_ids=true | all-gather | bytes 1105920 | tf_op jit(solution)/shard_map/all_gather | solution.py:86
  48.3 2.0 convert_element_type.159
  50.4 1.9 convert_reduce_fusion.2
  53.3 38.7 %all-gather = bf16[1,1,240,2048]{3,1,0,2:T(2,128)(2,1)S(1)} all-gather(bf16[1,1,30,2048]{3,1,0,2:T(2,128)(2,1)S(1)} %get-tuple-element.35), channel_id=2, replica_groups=mesh['section'=16,'tensor'=8] {'tensor'}, dimensions={2}, use_global_device_ids=true | all-gather | bytes 1105920 | tf_op jit(solution)/shard_map/all_gather | solution.py:85
  92.0 2.0 convert_element_type.156
  94.1 1.9 convert_reduce_fusion.3
  96.6 2.0 fusion.130
  98.8 39.1 %all-gather.3 = bf16[1,240,2048]{2,0,1:T(2,128)(2,1)S(1)} all-gather(bf16[1,30,2048]{2,0,1:T(2,128)(2,1)S(1)} %copy.44), channel_id=5, replica_groups=mesh['section'=16,'tensor'=8] {'tensor'}, dimensions={1}, use_global_device_ids=true | all-gather | bytes 1105920 | tf_op jit(solution)/shard_map/all_gather | solution.py:88
  138.5 1.5 multiply_convert_fusion.5
  143.0 2.0 fusion.128
  145.2 37.9 %all-gather.2 = bf16[1,240,2048]{2,0,1:T(2,128)(2,1)S(1)} all-gather(bf16[1,30,2048]{2,0,1:T(2,128)(2,1)S(1)} %copy.42), channel_id=4, replica_groups=mesh['section'=16,'tensor'=8] {'tensor'}, dimensions={1}, use_global_device_ids=true | all-gather | bytes 1105920 | tf_op jit(solution)/shard_map/all_gather | solution.py:87
  183.7 1.5 multiply_convert_fusion.3
  187.4 2.1 pad_maximum_fusion.1
  191.4 45.6 %all-gather.5 = bf16[1,1,240,2048]{3,1,0,2:T(2,128)(2,1)S(1)} all-gather(bf16[1,1,30,2048]{3,1,0,2:T(2,128)(2,1)S(1)} %get-tuple-element.36), channel_id=7, replica_groups=mesh['section'=16,'tensor'=8] {'tensor'}, dimensions={2}, use_global_device_ids=true | all-gather | bytes 1105920 | tf_op jit(solution)/shard_map/all_gather | solution.py:86
  238.6 2.3 fusion.126
  241.0 62.2 %all-reduce.5.cloned.1.call-done = f32[240,4096]{1,0:T(8,128)} async-done(((f32[240,4096]{1,0:T(8,128)}), f32[240,4096]{1,0:T(8,128)}) %all-reduce.5.cloned.1.call-update) | async-done | bytes 3932176
  303.2 1.6 dynamic-slice_reduce_fusion.1
  304.9 2.1 fusion.113
  307.0 1.4 collective-permute-start.1
  308.4 1.6 multiply_convert_fusion.4
  310.1 48.1 %all-gather.7 = bf16[8,30,2048]{2,1,0:T(8,128)(2,1)S(1)} all-gather(bf16[1,30,2048]{2,1,0:T(8,128)(2,1)S(1)} %fusion.123), channel_id=1, replica_groups=mesh['section'=16,'tensor'=8] {'tensor'}, dimensions={0}, use_global_device_ids=true | all-gather | bytes 1105920 | tf_op jit(solution)/shard_map/all_gather | solution.py:88
  359.4 3.1 fusion.76
  363.1 1.3 fusion.46
  368.0 14.6 %pad_maximum_fusion = bf16[2097152]{0:T(1024)(128)(2,1)S(1)} fusion(bf16[1048576]{0:T(1024)(128)(2,1)S(1)} %bitcast.178, bf16[1048576]{0:T(1024)(128)(2,1)S(1)} %bitcast.177), kind=kLoop, calls=%fused_computation | loop fusion | flops 8388608 | bytes 8388608 | tf_op jit(solution)/shard_map/concatenate | solution.py:140
  382.7 7.1 collective-permute-done.2
  389.8 4.7 collective-permute-start.3
  394.5 38.8 %all-gather.1 = bf16[1,1,240,2048]{3,1,0,2:T(2,128)(2,1)S(1)} all-gather(bf16[1,1,30,2048]{3,1,0,2:T(2,128)(2,1)S(1)} %copy-done.25), channel_id=3, replica_groups=mesh['section'=16,'tensor'=8] {'tensor'}, dimensions={2}, use_global_device_ids=true | all-gather | bytes 1105920 | tf_op jit(solution)/shard_map/all_gather | solution.py:85
  434.5 51.0 %collective-permute-done.3 = bf16[2097152]{0:T(1024)(128)(2,1)} collective-permute-done((bf16[2097152]{0:T(1024)(128)(2,1)S(1)}, bf16[2097152]{0:T(1024)(128)(2,1)}, u32[]{:S(2)}, u32[]{:S(2)}) %collective-permute-start.3) | collective-permute-done | bytes 4194336 | tf_op jit(solution)/shard_map/ppermute | solution.py:26
  485.5 3.2 collective-permute-start.4
  488.7 2.0 fusion.124
  492.0 1.6 multiply_convert_fusion.2
  494.7 35.9 %all-gather.6 = bf16[8,30,2048]{2,1,0:T(8,128)(2,1)S(1)} all-gather(bf16[1,30,2048]{2,1,0:T(8,128)(2,1)S(1)} %fusion.122), channel_id=1, replica_groups=mesh['section'=16,'tensor'=8] {'tensor'}, dimensions={0}, use_global_device_ids=true | all-gather | bytes 1105920 | tf_op jit(solution)/shard_map/all_gather | solution.py:87
  531.8 1.8 convolution_multiply_fusion
  536.4 2.1 pad_maximum_fusion.2
  538.5 40.9 %collective-permute-done.4 = bf16[2097152]{0:T(1024)(128)(2,1)} collective-permute-done((bf16[2097152]{0:T(1024)(128)(2,1)}, bf16[2097152]{0:T(1024)(128)(2,1)}, u32[]{:S(2)}, u32[]{:S(2)}) %collective-permute-start.4) | collective-permute-done | bytes 4194336 | tf_op jit(solution)/shard_map/ppermute | solution.py:26
  579.4 46.7 %collective-permute-start.5 = (bf16[2097152]{0:T(1024)(128)(2,1)}, bf16[2097152]{0:T(1024)(128)(2,1)}, u32[]{:S(2)}, u32[]{:S(2)}) collective-permute-start(bf16[2097152]{0:T(1024)(128)(2,1)} %collective-permute-done.4), channel_id=1, source_target_pairs={{0,64},{8,72},{16,80},{24,88},{32,96},{40,104},{48,112},{56,120},{... | collective-permute-start | bytes 12582920 | tf_op jit(solution)/shard_map/ppermute | solution.py:26
  626.3 5.0 fusion.30
  631.3 3.2 fusion.40
  634.5 96.2 %all-reduce.7.cloned.1.call-done = f32[240,4096]{1,0:T(8,128)} async-done(((f32[240,4096]{1,0:T(8,128)}), f32[240,4096]{1,0:T(8,128)}) %all-reduce.7.cloned.1.call-update) | async-done | bytes 3932176
  730.7 1.6 dynamic-slice_reduce_fusion.2
  732.3 2.4 fusion.115
  734.7 52.1 %collective-permute-done.5 = bf16[2097152]{0:T(1024)(128)(2,1)} collective-permute-done((bf16[2097152]{0:T(1024)(128)(2,1)}, bf16[2097152]{0:T(1024)(128)(2,1)}, u32[]{:S(2)}, u32[]{:S(2)}) %collective-permute-start.5) | collective-permute-done | bytes 4194336 | tf_op jit(solution)/shard_map/ppermute | solution.py:26
  786.9 6.0 slice_convert_fusion
  792.8 4.9 reshape.189
  797.8 4.9 reshape.188
  802.7 8.7 %convert_bitcast_fusion.2 = (bf16[1,512,2048]{2,1,0:T(8,128)(2,1)}, bf16[1,512,2048]{2,1,0:T(8,128)(2,1)}) fusion(f32[512,2048]{1,0:T(8,128)} %reshape.189, f32[512,2048]{1,0:T(8,128)} %fusion.40, bf16[1,512,2048]{2,1,0:T(8,128)(2,1)} %param.21, bf16[1,512,2048]{2,1,0:T(8,128)(2,1)} %param.17), kind=kLoop, calls=%fused_computation.41 | loop fusion | flops 10485760 | bytes 16777216 | tf_op jit(solution)/shard_map/broadcast_in_dim | solution.py:162
  812.5 3.6 convert_bitcast_fusion.3
  (136 shorter events, 25.6 us)
Async XLA Ops:
  7.2 131.3 %copy-start = (bf16[1,2048,512]{2,1,0:T(8,128)(2,1)S(1)}, bf16[1,2048,512]{2,1,0:T(8,128)(2,1)}, u32[]{:S(2)}) copy-start(bf16[1,2048,512]{2,1,0:T(8,128)(2,1)} %param.18) | copy-start | bytes 6291460
  7.2 296.0 %all-reduce.5.cloned.1.call-start = ((), (), s32[]{:S(2)}) async-start(), calls=%async_computation | async-start | bytes 7864320
  48.3 4.0 copy-start.23
  96.6 2.0 copy-start.26
  98.6 39.9 %copy-start.17 = (bf16[240,2048]{1,0:T(8,128)(2,1)}, bf16[240,2048]{1,0:T(8,128)(2,1)S(1)}, u32[]{:S(2)}) copy-start(bf16[240,2048]{1,0:T(8,128)(2,1)S(1)} %get-tuple-element.20) | copy-start | bytes 2949124
  138.5 1.5 copy-start.15
  138.5 2.0 copy-start.37
  141.6 0.8 copy-start.31
  143.0 2.0 copy-start.27
  145.0 38.6 %copy-start.14 = (bf16[240,2048]{1,0:T(8,128)(2,1)}, bf16[240,2048]{1,0:T(8,128)(2,1)S(1)}, u32[]{:S(2)}) copy-start(bf16[240,2048]{1,0:T(8,128)(2,1)S(1)} %get-tuple-element.18) | copy-start | bytes 2949124
  145.2 38.5 %copy-start.1 = (bf16[1,2048,512]{2,1,0:T(8,128)(2,1)S(1)}, bf16[1,2048,512]{2,1,0:T(8,128)(2,1)}, u32[]{:S(2)}) copy-start(bf16[1,2048,512]{2,1,0:T(8,128)(2,1)} %param.16) | copy-start | bytes 6291460
  183.6 1.5 copy-start.7
  183.7 2.0 copy-start.11
  186.6 0.8 copy-start.30
  189.6 541.2 %all-reduce.7.cloned.1.call-start = ((), (), s32[]{:S(2)}) async-start(), calls=%async_computation.1 | async-start | bytes 7864320
  237.0 1.2 copy-start.24
  238.6 71.4 %copy-start.10 = (bf16[1,30,2048]{2,0,1:T(2,128)(2,1)}, bf16[1,30,2048]{2,0,1:T(2,128)(2,1)S(1)}, u32[]{:S(2)}) copy-start(bf16[1,30,2048]{2,0,1:T(2,128)(2,1)S(1)} %get-tuple-element.33) | copy-start | bytes 368644
  303.2 5.2 copy-start.19
  307.0 3.0 collective-permute-start.1
  359.3 3.8 copy-start.18
  359.3 3.8 copy-start.20
  359.3 3.8 copy-start.32
  362.4 0.7 copy-start.33
  364.4 1.2 copy-start.16
  364.4 1.5 copy-start.22
  364.4 1.5 copy-start.40
  364.5 1.6 copy-start.41
  367.9 26.6 %copy-start.25 = (bf16[1,1,30,2048]{3,1,0,2:T(2,128)(2,1)S(1)}, bf16[1,1,30,2048]{3,1,0,2:T(2,128)(2,1)}, u32[]{:S(2)}) copy-start(bf16[1,1,30,2048]{3,1,0,2:T(2,128)(2,1)} %get-tuple-element.34) | copy-start | bytes 368644
  382.6 7.2 collective-permute-start.2
  389.8 95.7 %collective-permute-start.3 = (bf16[2097152]{0:T(1024)(128)(2,1)S(1)}, bf16[2097152]{0:T(1024)(128)(2,1)}, u32[]{:S(2)}, u32[]{:S(2)}) collective-permute-start(bf16[2097152]{0:T(1024)(128)(2,1)S(1)} %collective-permute-done.2), channel_id=1, source_target_pairs={{0,16},{8,24},{16,0},{24,8},{32,48},{40,56},{48,32},{56,40},{64,80... | collective-permute-start | bytes 12582920 | tf_op jit(solution)/shard_map/ppermute | solution.py:26
  434.5 56.2 %copy-start.36 = (bf16[30,2048]{1,0:T(8,128)(2,1)S(1)}, bf16[30,2048]{1,0:T(8,128)(2,1)}, u32[]{:S(2)}) copy-start(bf16[30,2048]{1,0:T(8,128)(2,1)} %get-tuple-element.30) | copy-start | bytes 368644
  434.5 57.5 %copy-start.2 = (bf16[1,2048,512]{2,1,0:T(8,128)(2,1)S(1)}, bf16[1,2048,512]{2,1,0:T(8,128)(2,1)}, u32[]{:S(2)}) copy-start(bf16[1,2048,512]{2,1,0:T(8,128)(2,1)} %param.16) | copy-start | bytes 6291460
  485.5 93.9 %collective-permute-start.4 = (bf16[2097152]{0:T(1024)(128)(2,1)}, bf16[2097152]{0:T(1024)(128)(2,1)}, u32[]{:S(2)}, u32[]{:S(2)}) collective-permute-start(bf16[2097152]{0:T(1024)(128)(2,1)} %collective-permute-done.3), channel_id=1, source_target_pairs={{0,32},{8,40},{16,48},{24,56},{32,0},{40,8},{48,16},{56,24},{64,96... | collective-permute-start | bytes 12582920 | tf_op jit(solution)/shard_map/ppermute | solution.py:26
  490.7 1.3 copy-start.21
  490.7 3.2 collective-permute-start
  531.8 1.8 copy-start.9
  531.8 2.0 copy-start.12
  531.8 2.1 copy-start.39
  533.9 1.8 copy-start.3
  534.9 0.7 copy-start.35
  579.4 207.4 %collective-permute-start.5 = (bf16[2097152]{0:T(1024)(128)(2,1)}, bf16[2097152]{0:T(1024)(128)(2,1)}, u32[]{:S(2)}, u32[]{:S(2)}) collective-permute-start(bf16[2097152]{0:T(1024)(128)(2,1)} %collective-permute-done.4), channel_id=1, source_target_pairs={{0,64},{8,72},{16,80},{24,88},{32,96},{40,104},{48,112},{56,120},{... | collective-permute-start | bytes 12582920 | tf_op jit(solution)/shard_map/ppermute | solution.py:26
  626.3 5.0 copy-start.8
  626.3 5.0 copy-start.29
  626.3 5.0 copy-start.34
  802.7 8.7 %copy-start.4 = (bf16[1,2048,512]{2,1,0:T(8,128)(2,1)S(1)}, bf16[1,2048,512]{2,1,0:T(8,128)(2,1)}, u32[]{:S(2)}) copy-start(bf16[1,2048,512]{2,1,0:T(8,128)(2,1)} %param.16) | copy-start | bytes 6291460
  802.7 8.7 %copy-start.5 = (f32[2048,512]{1,0:T(8,128)S(1)}, f32[2048,512]{1,0:T(8,128)}, u32[]{:S(2)}) copy-start(f32[2048,512]{1,0:T(8,128)} %reshape.188) | copy-start | bytes 12582916
  802.7 8.7 %copy-start.6 = (f32[2048,512]{1,0:T(8,128)S(1)}, f32[2048,512]{1,0:T(8,128)}, u32[]{:S(2)}) copy-start(f32[2048,512]{1,0:T(8,128)} %fusion.30) | copy-start | bytes 12582916
  802.7 9.8 %copy-start.13 = (bf16[1,2048,512]{2,1,0:T(8,128)(2,1)S(1)}, bf16[1,2048,512]{2,1,0:T(8,128)(2,1)}, u32[]{:S(2)}) copy-start(bf16[1,2048,512]{2,1,0:T(8,128)(2,1)} %param.20) | copy-start | bytes 6291460
  (2 other events, 1.3 us)
Sparse Core Ops, SparseCore 0:
  189.7 113.4 all-reduce.4
  538.6 192.0 all-reduce.6
where the time goes:
time: 832 us; the launch traced here: 823 us
  blocking collectives  324 us (39%)
  waiting for transfers between devices  310 us (37%)
  other arithmetic  64.9 us (8%)
  starting transfers between devices  57.5 us (7%)
  matrix products  27.1 us (3%)
  local copies, waits for them, and re-layouts  24.7 us (3%)
  between operations  15.6 us (2%)
    unnamed x4, waiting for transfers between devices  159 us
    ppermute x4, waiting for transfers between devices, partner(): return lax.ppermute(value, axis, pairs)  151 us
    all_gather x2, blocking collectives, body(): lax.all_gather(cotans[1], 'tensor', axis=0, tiled=True)  87.2 us
    all_gather x2, blocking collectives, body(): lax.all_gather(inputs_up[0, step_index], 'tensor', axis=0, tiled=True)  85.1 us
    all_gather x2, blocking collectives, body(): lax.all_gather(inputs_down[0, step_index], 'tensor', axis=0, tiled=True)  77.5 us
    all_gather x2, blocking collectives, body(): lax.all_gather(cotans[0], 'tensor', axis=0, tiled=True)  73.8 us
    ppermute x4, starting transfers between devices, partner(): return lax.ppermute(value, axis, pairs)  54.7 us
  transfers between devices with their start and end apart: 8, of which 7 were waited for; matrix products, arithmetic and copies ran while one was open for 4% of the time, Pallas kernels for 0%

commit v1 on v0

v1 whole, which is shorter than its diff:
```python
import functools

import jax
import jax.numpy as jnp
from jax import lax
from jax.experimental import pallas as pl
from jax.experimental.pallas import tpu as pltpu
from jax.sharding import PartitionSpec as P

D = 2048
FF = 4096
ROWS = 30
PAD = 32
HID = 512
TILE = 256
OPCOLS = 1024
MESH = pl.DeviceIdType.MESH

epsilon = 1e-05
learning_rate = 0.25
momentum_decay = 0.9
tanh_scale = 0.7978845608028654
cubic_term = 0.044715

N1U, C1U, N2U, C2U, N1D, C1D, N2D, C2D = range(8)
U1, U2, D1, D2 = range(4)
NT = D // TILE
NOP = OPCOLS // TILE
NGR = NT - NOP


def gelu_with_slope(preact):
    tanh_input = tanh_scale * (preact + cubic_term * preact * preact * preact)
    tangent = jnp.tanh(tanh_input)
    values = 0.5 * preact * (1.0 + tangent)
    slopes = 0.5 * (1.0 + tangent) + 0.5 * preact * (1.0 - tangent * tangent) * tanh_scale * (
        1.0 + 3.0 * cubic_term * preact * preact
    )
    return (values, slopes)


def dot_nt(a, b):
    return lax.dot_general(a, b, (((1,), (1,)), ((), ())), preferred_element_type=jnp.float32)


def dot_tn(a, b):
    return lax.dot_general(a, b, (((0,), (0,)), ((), ())), preferred_element_type=jnp.float32)


def kernel(
    in_down, in_up, g_down, g_up, loss,
    w1d_h, w2d_h, w1u_h, w2u_h, m1_h, m2_h,
    f_new, s_new, mo1, mo2, pass_d, pass_u,
    G, W1, W2, M1, M2, A, GP, PB, RR, ZB, NR, SC, CT, RL,
    MO, MG, MA, SF, SS, RF, RS,
    load_sem, out_sem, ag_s, ag_r, rs_s, rs_r, rl_s, rl_r, mo_s, mo_r, mg_s, mg_r, ma_s, ma_r,
    sf_s, sf_r, ss_s, ss_r,
):
    s = lax.axis_index("section")
    t = lax.axis_index("tensor")
    x = lax.rem(t, 4)
    zh = t // 4
    zo = 1 - zh

    def xpeer(k):
        return (s, zh * 4 + lax.rem(x + k, 4))

    zpeer = (s, zo * 4 + x)
    mirror = (15 - s, t)
    up = (lax.rem(s + 1, 16), t)
    down = (lax.rem(s + 15, 16), t)

    barrier = pltpu.get_barrier_semaphore()
    for peer in (xpeer(1), xpeer(2), xpeer(3), zpeer, mirror, up, down):
        pl.semaphore_signal(barrier, inc=1, device_id=peer, device_id_type=MESH)

    loads = []
    for i, (src, dst) in enumerate(
        ((w1u_h, W1.at[0]), (w2u_h, W2.at[0]), (w1d_h, W1.at[1]), (w2d_h, W2.at[1]), (m1_h, M1), (m2_h, M2))
    ):
        c = pltpu.make_async_copy(src.at[0], dst, load_sem.at[i])
        c.start()
        loads.append(c)

    def put_normed(ref, step, q, a):
        wide = ref[0, step].astype(jnp.float32)
        centred = wide - jnp.mean(wide, axis=-1, keepdims=True)
        inv = lax.rsqrt(jnp.mean(centred * centred, axis=-1, keepdims=True) + epsilon)
        NR[q, ROWS:PAD] = jnp.zeros((PAD - ROWS, D), jnp.float32)
        NR[q, 0:ROWS] = centred * inv
        SC[q, ROWS:PAD] = jnp.zeros((PAD - ROWS, 128), jnp.float32)
        SC[q, 0:ROWS] = jnp.broadcast_to(inv, (ROWS, 128))
        G[a, t] = NR[q].astype(jnp.bfloat16)

    def put_rows(value, a):
        CT[ROWS:PAD] = jnp.zeros((PAD - ROWS, D), jnp.float32)
        CT[0:ROWS] = value.astype(jnp.float32)
        G[a, t] = CT[...].astype(jnp.bfloat16)

    def rcopy(src, dst, ss, rs, dev):
        return pltpu.make_async_remote_copy(
            src_ref=src, dst_ref=dst, send_sem=ss, recv_sem=rs, device_id=dev, device_id_type=MESH
        )

    pending = []

    def send(src, dst, ss, rs, dev):
        c = rcopy(src, dst, ss, rs, dev)
        c.start()
        pending.append(c)

    def slot_send(a, slot, i, dev):
        send(G.at[a, slot], G.at[a, slot], ag_s.at[a, i], ag_r.at[a, i], dev)

    def slot_wait(a, slot, i):
        rcopy(G.at[a, slot], G.at[a, slot], ag_s.at[a, i], ag_r.at[a, i], zpeer).wait_recv()

    def from_x(k):
        return lax.rem(x + 4 - k, 4)

    def ag_z(a):
        slot_send(a, t, 0, zpeer)

    def ag_x(a):
        for k in (1, 3, 2):
            slot_send(a, t, k, xpeer(k))

    def ag_fwd(a):
        slot_wait(a, zo * 4 + x, 0)
        for k in (1, 3, 2):
            slot_send(a, zo * 4 + x, 4 + k, xpeer(k))

    def ag_wait(a):
        for k in (1, 3, 2):
            slot_wait(a, zh * 4 + from_x(k), k)
        for k in (1, 3, 2):
            slot_wait(a, zo * 4 + from_x(k), 4 + k)

    def ag_fwd_xf(a):
        for k in (1, 3, 2):
            slot_wait(a, zh * 4 + from_x(k), k)
            slot_send(a, zh * 4 + from_x(k), 4 + k, zpeer)

    def ag_wait_xf(a):
        slot_wait(a, zo * 4 + x, 0)
        for k in (1, 3, 2):
            slot_wait(a, zo * 4 + from_x(k), 4 + k)

    def hidden(q, w, an, ac):
        @pl.loop(0, HID // TILE)
        def _(j):
            cols = pl.ds(pl.multiple_of(j * TILE, TILE), TILE)
            n = G[an].reshape(8 * PAD, D)
            pre = jnp.dot(n, W1[w, :, cols], preferred_element_type=jnp.float32) * D ** (-0.5)
            values, slopes = gelu_with_slope(pre)
            A[q, :, cols] = values.astype(jnp.bfloat16)
            c = G[ac].reshape(8 * PAD, D)
            ga = dot_nt(c, W2[w, cols, :]) * FF ** (-0.5)
            GP[q, :, cols] = (ga * slopes).astype(jnp.bfloat16)

    def partial(q, w):
        @pl.loop(0, NT)
        def _(j):
            cols = pl.ds(pl.multiple_of(j * TILE, TILE), TILE)
            part = dot_nt(GP[q], W1[w, cols, :]) * D ** (-0.5)
            PB[q, :, :, cols] = part.astype(jnp.bfloat16).reshape(8, PAD, TILE)

    def rs_start(q):
        for k in (2, 1, 3):
            xk = lax.rem(x + k, 4)
            send(PB.at[q, zo * 4 + xk], RR.at[q, 4 + k], rs_s.at[q, 4 + k], rs_r.at[q, 4 + k], xpeer(k))
        for k in (2, 1, 3):
            xk = lax.rem(x + k, 4)
            send(PB.at[q, zh * 4 + xk], RR.at[q, k], rs_s.at[q, k], rs_r.at[q, k], xpeer(k))

    def rs_wait(q, i):
        rcopy(RR.at[q, i], RR.at[q, i], rs_s.at[q, i], rs_r.at[q, i], zpeer).wait_recv()

    def rs_mid(q):
        for k in (1, 3, 2):
            rs_wait(q, 4 + k)
        total = PB[q, zo * 4 + x].astype(jnp.float32)
        for k in (1, 2, 3):
            total = total + RR[q, 4 + k].astype(jnp.float32)
        ZB[q] = total.astype(jnp.bfloat16)
        send(ZB.at[q], RR.at[q, 0], rs_s.at[q, 0], rs_r.at[q, 0], zpeer)

    def rs_end(q, ac):
        for k in (1, 3, 2):
            rs_wait(q, k)
        total = PB[q, t].astype(jnp.float32)
        for k in (1, 2, 3):
            total = total + RR[q, k].astype(jnp.float32)
        rs_wait(q, 0)
        gn = total + RR[q, 0].astype(jnp.float32)
        normed = NR[q]
        first_mean = jnp.mean(gn, axis=-1, keepdims=True)
        second_mean = jnp.mean(gn * normed, axis=-1, keepdims=True)
        return G[ac, t].astype(jnp.float32) + SC[q, :, 0:1] * (gn - first_mean - normed * second_mean)

    def relay(q, ac, i, a, dev):
        RL[i] = rs_end(q, ac).astype(jnp.bfloat16)
        send(RL.at[i], G.at[a, t], rl_s.at[i], rl_r.at[i], dev)

    def relay_wait(i, a, edge, row):
        rcopy(RL.at[i], G.at[a, t], rl_s.at[i], rl_r.at[i], zpeer).wait_recv()

        @pl.when(s == edge)
        def _():
            put_rows(loss[row], a)

    def mirror_cols(a):
        send(G.at[a, :, :, 0:OPCOLS], MO.at[a], mo_s.at[a], mo_r.at[a], mirror)

    def mirror_hidden(q):
        send(GP.at[q], MG.at[q], mg_s.at[q], mg_r.at[q], mirror)
        send(A.at[q], MA.at[q], ma_s.at[q], ma_r.at[q], mirror)

    def flat(ref, a, cols):
        return ref[a, :, :, cols].reshape(8 * PAD, TILE)

    put_rows(g_up[0], C1U)
    put_normed(in_up, 0, U1, N1U)
    pl.semaphore_wait(barrier, 7)
    ag_z(C1U)
    ag_x(N1U)
    ag_x(C1U)
    ag_z(N1U)
    put_normed(in_up, 1, U2, N2U)
    put_normed(in_down, 0, D1, N1D)
    put_rows(g_down[0], C1D)
    put_normed(in_down, 1, D2, N2D)
    ag_fwd(C1U)
    ag_fwd_xf(N1U)
    ag_z(N2U)
    loads[0].wait()
    loads[1].wait()
    ag_wait(C1U)
    ag_wait_xf(N1U)
    ag_z(N1D)
    ag_z(C1D)
    mirror_cols(C1U)
    mirror_cols(N1U)
    ag_x(N2U)
    ag_fwd(N2U)
    hidden(U1, 0, N1U, C1U)
    partial(U1, 0)
    rs_start(U1)
    mirror_hidden(U1)
    ag_z(N2D)
    ag_wait(N2U)
    mirror_cols(N2U)
    rs_mid(U1)
    ag_x(N1D)
    relay(U1, C1U, 0, C2U, up)
    ag_fwd(N1D)
    relay_wait(0, C2U, 0, 1)
    ag_z(C2U)
    ag_x(C2U)
    ag_x(C1D)
    ag_fwd(C2U)
    ag_fwd(C1D)
    loads[2].wait()
    loads[3].wait()
    ag_wait(C2U)
    hidden(U2, 0, N2U, C2U)
    mirror_hidden(U2)
    mirror_cols(C2U)

    for j in range(NGR):
        cols = pl.ds(OPCOLS + j * TILE, TILE)
        gf = dot_tn(flat(G, N1U, cols), GP[U1]) + dot_tn(flat(G, N2U, cols), GP[U2])
        SF[j] = (gf * D ** (-0.5)).astype(jnp.bfloat16)
        send(SF.at[j], RF.at[j], sf_s.at[j], sf_r.at[j], mirror)
        gs = dot_tn(A[U1], flat(G, C1U, cols)) + dot_tn(A[U2], flat(G, C2U, cols))
        SS[j] = (gs * FF ** (-0.5)).astype(jnp.bfloat16)
        send(SS.at[j], RS.at[j], ss_s.at[j], ss_r.at[j], mirror)

    ag_wait(N1D)
    ag_wait(C1D)
    hidden(D1, 1, N1D, C1D)
    partial(D1, 1)
    rs_start(D1)
    ag_x(N2D)
    ag_fwd(N2D)
    partial(U2, 0)
    rs_mid(D1)
    relay(D1, C1D, 1, C2D, down)
    rs_start(U2)
    relay_wait(1, C2D, 15, 0)
    ag_z(C2D)
    ag_x(C2D)
    ag_fwd(C2D)
    rs_mid(U2)
    ag_wait(N2D)
    ag_wait(C2D)
    hidden(D2, 1, N2D, C2D)
    partial(D2, 1)
    rs_start(D2)

    CT[...] = rs_end(U2, C2U)
    pass_u[0] = CT[0:ROWS].astype(jnp.bfloat16)

    loads[4].wait()
    loads[5].wait()
    outs = []

    def update(j, first_mirror, second_mirror):
        cols = pl.ds(j * TILE, TILE)
        gf = dot_tn(flat(G, N1D, cols), GP[D1]) + dot_tn(flat(G, N2D, cols), GP[D2])
        moment = momentum_decay * M1[cols, :].astype(jnp.float32) + gf * D ** (-0.5) + first_mirror()
        M1[cols, :] = moment.astype(jnp.bfloat16)
        W1[1, cols, :] = (W1[1, cols, :].astype(jnp.float32) - learning_rate * moment).astype(jnp.bfloat16)
        gs = dot_tn(A[D1], flat(G, C1D, cols)) + dot_tn(A[D2], flat(G, C2D, cols))
        moment = momentum_decay * M2[:, cols].astype(jnp.float32) + gs * FF ** (-0.5) + second_mirror()
        M2[:, cols] = moment.astype(jnp.bfloat16)
        W2[1, :, cols] = (W2[1, :, cols].astype(jnp.float32) - learning_rate * moment).astype(jnp.bfloat16)
        for i, (src, dst) in enumerate((
            (W1.at[1, cols, :], f_new.at[0, cols, :]),
            (M1.at[cols, :], mo1.at[0, cols, :]),
            (W2.at[1, :, cols], s_new.at[0, :, cols]),
            (M2.at[:, cols], mo2.at[0, :, cols]),
        )):
            c = pltpu.make_async_copy(src, dst, out_sem.at[j, i])
            c.start()
            outs.append(c)

    for q in (U1, U2):
        rcopy(GP.at[q], MG.at[q], mg_s.at[q], mg_r.at[q], mirror).wait_recv()
        rcopy(A.at[q], MA.at[q], ma_s.at[q], ma_r.at[q], mirror).wait_recv()
    for a in (N1U, C1U, N2U, C2U):
        rcopy(MO.at[a], MO.at[a], mo_s.at[a], mo_r.at[a], mirror).wait_recv()
    for j in range(NOP):
        cols = pl.ds(j * TILE, TILE)
        update(
            j,
            lambda: (dot_tn(flat(MO, N1U, cols), MG[U1]) + dot_tn(flat(MO, N2U, cols), MG[U2])) * D ** (-0.5),
            lambda: (dot_tn(MA[U1], flat(MO, C1U, cols)) + dot_tn(MA[U2], flat(MO, C2U, cols))) * FF ** (-0.5),
        )
    rs_mid(D2)
    for j in range(NGR):
        rcopy(SF.at[j], RF.at[j], sf_s.at[j], sf_r.at[j], mirror).wait_recv()
        rcopy(SS.at[j], RS.at[j], ss_s.at[j], ss_r.at[j], mirror).wait_recv()
        update(
            NOP + j,
            lambda: RF[j].astype(jnp.float32),
            lambda: RS[j].astype(jnp.float32),
        )
    CT[...] = rs_end(D2, C2D)
    pass_d[0] = CT[0:ROWS].astype(jnp.bfloat16)
    for c in pending:
        c.wait_send()
    for c in outs:
        c.wait()


def body(*blocks):
    bf16, f32 = jnp.bfloat16, jnp.float32
    dma = pltpu.SemaphoreType.DMA
    vmem = pl.BlockSpec(memory_space=pltpu.VMEM)
    hbm = pl.BlockSpec(memory_space=pl.ANY)
    return pl.pallas_call(
        kernel,
        out_shape=(
            jax.ShapeDtypeStruct((1, D, HID), bf16),
            jax.ShapeDtypeStruct((1, HID, D), bf16),
            jax.ShapeDtypeStruct((1, D, HID), bf16),
            jax.ShapeDtypeStruct((1, HID, D), bf16),
            jax.ShapeDtypeStruct((1, ROWS, D), bf16),
            jax.ShapeDtypeStruct((1, ROWS, D), bf16),
        ),
        in_specs=[vmem] * 5 + [hbm] * 6,
        out_specs=[hbm] * 4 + [vmem] * 2,
        scratch_shapes=[
            pltpu.VMEM((8, 8, PAD, D), bf16),
            pltpu.VMEM((2, D, HID), bf16),
            pltpu.VMEM((2, HID, D), bf16),
            pltpu.VMEM((D, HID), bf16),
            pltpu.VMEM((HID, D), bf16),
            pltpu.VMEM((4, 8 * PAD, HID), bf16),
            pltpu.VMEM((4, 8 * PAD, HID), bf16),
            pltpu.VMEM((4, 8, PAD, D), bf16),
            pltpu.VMEM((4, 8, PAD, D), bf16),
            pltpu.VMEM((4, PAD, D), bf16),
            pltpu.VMEM((4, PAD, D), f32),
            pltpu.VMEM((4, PAD, 128), f32),
            pltpu.VMEM((PAD, D), f32),
            pltpu.VMEM((2, PAD, D), bf16),
            pltpu.VMEM((4, 8, PAD, OPCOLS), bf16),
            pltpu.VMEM((2, 8 * PAD, HID), bf16),
            pltpu.VMEM((2, 8 * PAD, HID), bf16),
            pltpu.VMEM((NGR, TILE, HID), bf16),
            pltpu.VMEM((NGR, HID, TILE), bf16),
            pltpu.VMEM((NGR, TILE, HID), bf16),
            pltpu.VMEM((NGR, HID, TILE), bf16),
            dma((6,)), dma((NT, 4)),
            dma((8, 8)), dma((8, 8)),
            dma((4, 8)), dma((4, 8)),
            dma((2,)), dma((2,)),
            dma((4,)), dma((4,)),
            dma((2,)), dma((2,)), dma((2,)), dma((2,)),
            dma((NGR,)), dma((NGR,)), dma((NGR,)), dma((NGR,)),
        ],
        compiler_params=pltpu.CompilerParams(
            collective_id=0, has_side_effects=True, vmem_limit_bytes=60 * 2**20
        ),
        cost_estimate=pl.CostEstimate(flops=12 * 10**9, bytes_accessed=21 * 10**6, transcendentals=10**6),
        name="relay_backward",
    )(*blocks)


def solution(mesh):
    placed = (
        P("section", None, "tensor", None),
        P("section", None, "tensor", None),
        P("section", "tensor", None),
        P("section", "tensor", None),
        P(None, "tensor", None),
        P("section", None, "tensor"),
        P("section", "tensor", None),
        P("section", None, "tensor"),
        P("section", "tensor", None),
        P("section", None, "tensor"),
        P("section", "tensor", None),
    )
    return jax.shard_map(
        body,
        mesh=mesh,
        in_specs=placed,
        out_specs=(
            P("section", None, "tensor"),
            P("section", "tensor", None),
            P("section", None, "tensor"),
            P("section", "tensor", None),
            P("section", "tensor", None),
            P("section", "tensor", None),
        ),
        check_vma=False,
    )
```

time: 832 us -> 250 us (0.30)
  blocking collectives: 324 us -> 0 us
  waiting for transfers between devices: 310 us -> 0 us
  Pallas kernels: 0 us -> 229 us
  other arithmetic: 64.9 us -> 0 us
  starting transfers between devices: 57.5 us -> 0 us
  matrix products: 27.1 us -> 0 us
  between operations: 15.6 us -> 0.66 us
  local copies, waits for them, and re-layouts: 24.7 us -> 15.7 us
    all_gather x8 -> x0, blocking collectives: 324 us -> none  [the longest x2 87.2 us: body(): lax.all_gather(cotans[1], 'tensor', axis=0, tiled=True)]
    pallas_call x0 -> x1, Pallas kernels: none -> 229 us  [body(): pl.pallas_call(kernel, out_shape=(jax.ShapeDtypeStruct((1, D, HID), bf16)...]
    unnamed x4 -> x0, waiting for transfers between devices: 159 us -> none
    ppermute x6 -> x0, waiting for transfers between devices: 151 us -> none  [the longest x4 151 us: partner(): return lax.ppermute(value, axis, pairs)]
    ppermute x6 -> x0, starting transfers between devices: 57.4 us -> none  [the longest x4 54.7 us: partner(): return lax.ppermute(value, axis, pairs)]
    dot_general x16 -> x0, matrix products: 27.1 us -> none  [the longest x4 10.8 us: contract_rows(): lax.dot_general(left_side, right_side, (((0,), (0,)), ((), ())), preferre...]
    convert_element_type x8 -> x0, other arithmetic: 20.3 us -> none  [the longest x4 8.23 us: body(): normed_low = normed.astype(jnp.bfloat16)]
    concatenate x3 -> x0, other arithmetic: 18.9 us -> none  [the longest x1 14.6 us: body(): jnp.concatenate([up_first.astype(jnp.bfloat16).reshape(-1), up_second.ast...]
  transfers between devices with their start and end apart: 8 -> 0, of which waited for: 7 -> 0; matrix products, arithmetic and copies ran while one was open for 4% -> 0% of each run, Pallas kernels for 0% -> 0%
where the time goes in v1:
time: 250 us; the launch traced here: 245 us
  Pallas kernels  229 us (92%)
  local copies, waits for them, and re-layouts  15.7 us (6%)
    pallas_call x1, Pallas kernels, body(): pl.pallas_call(kernel, out_shape=(jax.ShapeDtypeStruct((1, D, HID), bf16)...  229 us
    unnamed x19, local copies, waits for them, and re-layouts  15.7 us

profile of v1, /device:TPU:0, one launch (start us, length us, event | category | flops | bytes accessed | tf_op | source)
XLA Modules:
  0.0 244.9 jit_solution(4276553951046553740)
XLA Ops:
  0.6 1.7 copy.17.in_down
  2.4 1.7 copy.18.in_up
  4.1 1.7 copy.19.loss
  5.8 228.5 %relay_backward.1 = (bf16[1,2048,512]{2,1,0:T(8,128)(2,1)}, bf16[1,512,2048]{2,1,0:T(8,128)(2,1)}, bf16[1,2048,512]{2,1,0:T(8,128)(2,1)}, bf16[1,512,2048]{2,1,0...) custom-call(bf16[1,2,30,2048]{3,2,1,0:T(8,128)(2,1)} %copy.17.in_down, ...), custom_call_target="tpu_custom_call" | custom-call | flops 12000000000 | bytes 21000000 | tf_op jit(solution)/shard_map/relay_backward/pallas_call | solution.py:362
  234.3 0.0 copy-start.2
  234.3 3.2 %copy.26 = bf16[1,2048,512]{2,1,0:T(8,128)(2,1)} copy(bf16[1,2048,512]{2,1,0:T(8,128)(2,1)} %get-tuple-element.12) | data formatting | bytes 4194304
  237.5 0.0 copy-done.2
  237.5 0.0 copy-start.1
  237.5 1.3 copy.27
  238.9 1.0 copy-done.1
  239.9 0.0 copy-start
  239.9 1.3 copy.28
  241.2 1.0 copy-done
  242.2 0.0 copy-start.4
  242.2 0.0 copy-start.3
  242.2 1.3 copy.29
  243.6 0.0 copy-done.4
  243.6 0.7 copy.30
  244.2 0.0 copy-done.3
  244.2 0.7 copy.31
Async XLA Ops:
  234.3 3.2 %copy-start.2 = (bf16[1,512,2048]{2,1,0:T(8,128)(2,1)S(1)}, bf16[1,512,2048]{2,1,0:T(8,128)(2,1)}, u32[]{:S(2)}) copy-start(bf16[1,512,2048]{2,1,0:T(8,128)(2,1)} %get-tuple-element.13) | copy-start | bytes 6291460
  237.5 2.3 copy-start.1
  239.9 2.3 copy-start
  242.2 1.3 copy-start.4
  242.2 2.0 copy-start.3

commit v2 on v1

v2 whole, which is shorter than its diff:
```python
import functools

import jax
import jax.numpy as jnp
from jax import lax
from jax.experimental import pallas as pl
from jax.experimental.pallas import tpu as pltpu
from jax.sharding import PartitionSpec as P

D = 2048
FF = 4096
ROWS = 30
PAD = 32
HID = 512
TILE = 256
MESH = pl.DeviceIdType.MESH

epsilon = 1e-05
learning_rate = 0.25
momentum_decay = 0.9
tanh_scale = 0.7978845608028654
cubic_term = 0.044715

N1U, C1U, N2U, C2U, N1D, C1D, N2D, C2D, N1M, C1M, N2M, C2M = range(12)
U1, U2, D1, D2 = range(4)
NT = D // TILE
HALF = PAD // 2
MODES = (0, 0, 0, 0, 0, 1, 1, 1, 1, 0, 0, 1)
ORDER = (
    (0, N1D), (0, C1D), (0, N2U), (1, N1D), (1, C1D), (0, N1M), (2, N1D), (2, C1D), (1, N2U), (0, N2D), (1, N1M),
    (2, N2U), (0, C1M), (0, C2M), (0, N2M), (1, C1M), (1, N2M), (1, N2D), (2, N1M), (2, C1M), (2, N2M), (2, N2D),
    (1, C2M), (2, C2M),
)
FILLS = (2, 1, 0, 2, 3, 2, 2, 3, 0, 3, 1, 3, 0, 1, 0, 25, 20)


def gelu_with_slope(preact):
    tanh_input = tanh_scale * (preact + cubic_term * preact * preact * preact)
    tangent = jnp.tanh(tanh_input)
    values = 0.5 * preact * (1.0 + tangent)
    slopes = 0.5 * (1.0 + tangent) + 0.5 * preact * (1.0 - tangent * tangent) * tanh_scale * (
        1.0 + 3.0 * cubic_term * preact * preact
    )
    return (values, slopes)


def dot_nt(a, b):
    return lax.dot_general(a, b, (((1,), (1,)), ((), ())), preferred_element_type=jnp.float32)


def dot_tn(a, b):
    return lax.dot_general(a, b, (((0,), (0,)), ((), ())), preferred_element_type=jnp.float32)


def kernel(
    in_down, in_up, g_down, g_up, loss, w1d_h, w2d_h, w1u_h, w2u_h,
    t1_h, t2_h, pass_d, pass_u,
    G, W1, W2, A, GP, PB, RR, ZB, NR, SC, CT, RL, MG, MA, ACC1, ACC2, T1, T2,
    load_sem, out_sem, ag_s, ag_r, rs_s, rs_r, rl_s, rl_r, row_s, row_r, mg_s, mg_r, ma_s, ma_r,
):
    s = lax.axis_index("section")
    t = lax.axis_index("tensor")
    x = lax.rem(t, 4)
    zh = t // 4
    zo = 1 - zh

    def xpeer(k):
        return (s, zh * 4 + lax.rem(x + k, 4))

    zpeer = (s, zo * 4 + x)
    mirror = (15 - s, t)
    up = (lax.rem(s + 1, 16), t)
    down = (lax.rem(s + 15, 16), t)

    barrier = pltpu.get_barrier_semaphore()
    for peer in (xpeer(1), xpeer(2), xpeer(3), zpeer, mirror, up, down):
        pl.semaphore_signal(barrier, inc=1, device_id=peer, device_id_type=MESH)

    loads = []
    for i, (src, dst) in enumerate(
        ((w1u_h, W1.at[0]), (w2u_h, W2.at[0]), (w1d_h, W1.at[1]), (w2d_h, W2.at[1]))
    ):
        c = pltpu.make_async_copy(src.at[0], dst, load_sem.at[i])
        c.start()
        loads.append(c)

    def put_normed(ref, step, q, a):
        wide = ref[0, step].astype(jnp.float32)
        centred = wide - jnp.mean(wide, axis=-1, keepdims=True)
        inv = lax.rsqrt(jnp.mean(centred * centred, axis=-1, keepdims=True) + epsilon)
        NR[q, ROWS:PAD] = jnp.zeros((PAD - ROWS, D), jnp.float32)
        NR[q, 0:ROWS] = centred * inv
        SC[q, ROWS:PAD] = jnp.zeros((PAD - ROWS, 128), jnp.float32)
        SC[q, 0:ROWS] = jnp.broadcast_to(inv, (ROWS, 128))
        G[a, t] = NR[q].astype(jnp.bfloat16)

    def put_rows(value, a):
        CT[ROWS:PAD] = jnp.zeros((PAD - ROWS, D), jnp.float32)
        CT[0:ROWS] = value.astype(jnp.float32)
        G[a, t] = CT[...].astype(jnp.bfloat16)

    def rcopy(src, dst, ss, rs, dev):
        return pltpu.make_async_remote_copy(
            src_ref=src, dst_ref=dst, send_sem=ss, recv_sem=rs, device_id=dev, device_id_type=MESH
        )

    pending = []

    def send(src, dst, ss, rs, dev):
        c = rcopy(src, dst, ss, rs, dev)
        c.start()
        pending.append(c)

    waited = set()

    def ag_ref(a, slot, half=None):
        return G.at[a, slot] if half is None else G.at[a, slot, pl.ds(half * HALF, HALF)]

    def ag_send(a, i, dev, slot, half=None):
        ref = ag_ref(a, slot, half)
        send(ref, ref, ag_s.at[a, i], ag_r.at[a, i], dev)

    def near(k):
        return zh * 4 + lax.rem(x + k, 4)

    def far(k):
        return zo * 4 + lax.rem(x + k, 4)

    def landing(a, i):
        first = MODES[a] == 0
        return (
            (far(0), None), (near(3), None), (near(1), None), (near(2), 0), (near(2), 1),
            (far(3), None), (far(1), None),
            (far(2), 0 if first else None), (far(2), 1),
        )[i]

    def ag_wait(a, *which):
        for i in which:
            if (a, i) not in waited:
                waited.add((a, i))
                ref = ag_ref(a, *landing(a, i))
                rcopy(ref, ref, ag_s.at[a, i], ag_r.at[a, i], zpeer).wait_recv()

    def ag_done(a):
        ag_wait(a, *range(9 if MODES[a] == 0 else 8))

    def row_wait(i):
        ref = G.at[N1M + i, t]
        rcopy(ref, ref, row_s.at[i], row_r.at[i], mirror).wait_recv()

    def stage(a, k):
        first = MODES[a] == 0
        if k == 0:
            if a >= N1M:
                row_wait(a - N1M)
            if first:
                ag_send(a, 0, zpeer, t)
            ag_send(a, 1, xpeer(1), t)
            ag_send(a, 2, xpeer(3), t)
            if not first:
                ag_send(a, 0, zpeer, t)
        elif k == 1:
            ag_wait(a, 1)
            ag_send(a, 3, xpeer(1), near(3), 0)
            if not first:
                ag_send(a, 5, zpeer, near(3))
            ag_wait(a, 2)
            ag_send(a, 4, xpeer(3), near(1), 1)
            if not first:
                ag_send(a, 6, zpeer, near(1))
            else:
                ag_wait(a, 0)
                ag_send(a, 5, xpeer(1), far(0))
                ag_send(a, 6, xpeer(3), far(0))
        elif first:
            ag_wait(a, 5)
            ag_send(a, 7, xpeer(1), far(3), 0)
            ag_wait(a, 6)
            ag_send(a, 8, xpeer(3), far(1), 1)
        else:
            ag_wait(a, 3, 4)
            ag_send(a, 7, zpeer, near(2))

    def row(a):
        send(G.at[a, t], G.at[N1M + a, t], row_s.at[a], row_r.at[a], mirror)

    queue = list(ORDER)
    fills = list(FILLS)
    ready = {N1M, C1M, N2M}

    def run_next():
        k, a = queue.pop(0)
        stage(a, k)

    def fill():
        for _ in range(fills.pop(0)):
            if queue and (queue[0][1] < N1M or queue[0][1] in ready):
                run_next()

    def need(*arrays):
        while any(a in arrays for _, a in queue):
            run_next()
        for a in arrays:
            ag_done(a)

    def hidden(q, w, an, ac):
        @pl.loop(0, HID // TILE)
        def _(j):
            cols = pl.ds(pl.multiple_of(j * TILE, TILE), TILE)
            n = G[an].reshape(8 * PAD, D)
            pre = jnp.dot(n, W1[w, :, cols], preferred_element_type=jnp.float32) * D ** (-0.5)
            values, slopes = gelu_with_slope(pre)
            A[q, :, cols] = values.astype(jnp.bfloat16)
            c = G[ac].reshape(8 * PAD, D)
            ga = dot_nt(c, W2[w, cols, :]) * FF ** (-0.5)
            GP[q, :, cols] = (ga * slopes).astype(jnp.bfloat16)

    def partial(q, w):
        @pl.loop(0, NT)
        def _(j):
            cols = pl.ds(pl.multiple_of(j * TILE, TILE), TILE)
            part = dot_nt(GP[q], W1[w, cols, :]) * D ** (-0.5)
            PB[q, :, :, cols] = part.astype(jnp.bfloat16).reshape(8, PAD, TILE)

    def rs_start(q):
        for k in (2, 1, 3):
            send(PB.at[q, far(k)], RR.at[q, 4 + k], rs_s.at[q, 4 + k], rs_r.at[q, 4 + k], xpeer(k))
        for k in (2, 1, 3):
            send(PB.at[q, near(k)], RR.at[q, k], rs_s.at[q, k], rs_r.at[q, k], xpeer(k))

    def rs_wait(q, i):
        rcopy(RR.at[q, i], RR.at[q, i], rs_s.at[q, i], rs_r.at[q, i], zpeer).wait_recv()

    def rs_mid(q):
        for k in (1, 3, 2):
            rs_wait(q, 4 + k)
        total = PB[q, far(0)].astype(jnp.float32)
        for k in (1, 2, 3):
            total = total + RR[q, 4 + k].astype(jnp.float32)
        ZB[q] = total.astype(jnp.bfloat16)
        send(ZB.at[q], RR.at[q, 0], rs_s.at[q, 0], rs_r.at[q, 0], zpeer)

    def rs_end(q, ac):
        for k in (1, 3, 2):
            rs_wait(q, k)
        total = PB[q, t].astype(jnp.float32)
        for k in (1, 2, 3):
            total = total + RR[q, k].astype(jnp.float32)
        rs_wait(q, 0)
        gn = total + RR[q, 0].astype(jnp.float32)
        normed = NR[q]
        first_mean = jnp.mean(gn, axis=-1, keepdims=True)
        second_mean = jnp.mean(gn * normed, axis=-1, keepdims=True)
        return G[ac, t].astype(jnp.float32) + SC[q, :, 0:1] * (gn - first_mean - normed * second_mean)

    def relay(q, ac, i, a, dev):
        RL[i] = rs_end(q, ac).astype(jnp.bfloat16)
        send(RL.at[i], G.at[a, t], rl_s.at[i], rl_r.at[i], dev)

    def relay_wait(i, a, edge, which):
        rcopy(RL.at[i], G.at[a, t], rl_s.at[i], rl_r.at[i], zpeer).wait_recv()

        @pl.when(s == edge)
        def _():
            put_rows(loss[which], a)

    def mirror_hidden(q):
        send(GP.at[q], MG.at[q], mg_s.at[q], mg_r.at[q], mirror)
        send(A.at[q], MA.at[q], ma_s.at[q], ma_r.at[q], mirror)

    def mirror_wait(q):
        rcopy(GP.at[q], MG.at[q], mg_s.at[q], mg_r.at[q], mirror).wait_recv()
        rcopy(A.at[q], MA.at[q], ma_s.at[q], ma_r.at[q], mirror).wait_recv()

    def flat(a, cols):
        return G[a, :, :, cols].reshape(8 * PAD, TILE)

    def out_copies(j):
        cols = pl.ds(pl.multiple_of(j * TILE, TILE), TILE)
        return (
            pltpu.make_async_copy(T1.at[cols, :], t1_h.at[cols, :], out_sem.at[0, j]),
            pltpu.make_async_copy(T2.at[:, cols], t2_h.at[:, cols], out_sem.at[1, j]),
        )

    def add_terms(terms, first=False, last=False):
        @pl.loop(0, NT)
        def _(j):
            cols = pl.ds(pl.multiple_of(j * TILE, TILE), TILE)
            one = sum(dot_tn(flat(n, cols), gp[q]) for n, c, gp, ac, q in terms)
            two = sum(dot_tn(ac[q], flat(c, cols)) for n, c, gp, ac, q in terms)
            if not first:
                one = one + ACC1[cols, :]
                two = two + ACC2[:, cols]
            if last:
                T1[cols, :] = (one * D ** (-0.5)).astype(jnp.bfloat16)
                T2[:, cols] = (two * FF ** (-0.5)).astype(jnp.bfloat16)
                for c in out_copies(j):
                    c.start()
            else:
                ACC1[cols, :] = one
                ACC2[:, cols] = two

    put_rows(g_up[0], C1U)
    put_normed(in_up, 0, U1, N1U)
    pl.semaphore_wait(barrier, 7)
    row(C1U)
    row(N1U)
    stage(N1U, 0)
    stage(C1U, 0)
    put_normed(in_down, 0, D1, N1D)
    put_rows(g_down[0], C1D)
    put_normed(in_up, 1, U2, N2U)
    put_normed(in_down, 1, D2, N2D)
    row(N2U)
    stage(N1U, 1)
    stage(C1U, 1)
    stage(N1U, 2)
    stage(C1U, 2)
    fill()
    loads[0].wait()
    loads[1].wait()
    ag_done(N1U)
    ag_done(C1U)
    fill()
    hidden(U1, 0, N1U, C1U)
    partial(U1, 0)
    rs_start(U1)
    mirror_hidden(U1)
    fill()
    rs_mid(U1)
    fill()
    relay(U1, C1U, 0, C2U, up)
    fill()
    relay_wait(0, C2U, 0, 1)
    stage(C2U, 0)
    row(C2U)
    ready.add(C2M)
    fill()
    stage(C2U, 1)
    fill()
    stage(C2U, 2)
    fill()
    need(N2U)
    ag_done(C2U)
    hidden(U2, 0, N2U, C2U)
    mirror_hidden(U2)
    need(N1D, C1D)
    loads[2].wait()
    loads[3].wait()
    hidden(D1, 1, N1D, C1D)
    partial(D1, 1)
    rs_start(D1)
    fill()
    partial(U2, 0)
    add_terms([(N1D, C1D, GP, A, D1)], first=True)
    rs_mid(D1)
    fill()
    relay(D1, C1D, 1, C2D, down)
    fill()
    relay_wait(1, C2D, 15, 0)
    stage(C2D, 0)
    fill()
    stage(C2D, 1)
    fill()
    rs_start(U2)
    stage(C2D, 2)
    fill()
    need(N2D)
    ag_done(C2D)
    hidden(D2, 1, N2D, C2D)
    partial(D2, 1)
    rs_start(D2)
    fill()
    rs_mid(U2)
    fill()
    need(N1M, C1M)
    mirror_wait(U1)
    add_terms([(N2D, C2D, GP, A, D2), (N1M, C1M, MG, MA, U1)])
    CT[...] = rs_end(U2, C2U)
    pass_u[0] = CT[0:ROWS].astype(jnp.bfloat16)
    rs_mid(D2)
    need(N2M, C2M)
    mirror_wait(U2)
    add_terms([(N2M, C2M, MG, MA, U2)], last=True)
    CT[...] = rs_end(D2, C2D)
    pass_d[0] = CT[0:ROWS].astype(jnp.bfloat16)
    for c in pending:
        c.wait_send()

    @pl.loop(0, NT)
    def _(j):
        for c in out_copies(j):
            c.wait()


def backward(*blocks):
    bf16, f32 = jnp.bfloat16, jnp.float32
    dma = pltpu.SemaphoreType.DMA
    vmem = pl.BlockSpec(memory_space=pltpu.VMEM)
    hbm = pl.BlockSpec(memory_space=pl.ANY)
    return pl.pallas_call(
        kernel,
        out_shape=(
            jax.ShapeDtypeStruct((D, HID), bf16),
            jax.ShapeDtypeStruct((HID, D), bf16),
            jax.ShapeDtypeStruct((1, ROWS, D), bf16),
            jax.ShapeDtypeStruct((1, ROWS, D), bf16),
        ),
        in_specs=[vmem] * 5 + [hbm] * 4,
        out_specs=[hbm] * 2 + [vmem] * 2,
        scratch_shapes=[
            pltpu.VMEM((12, 8, PAD, D), bf16),
            pltpu.VMEM((2, D, HID), bf16),
            pltpu.VMEM((2, HID, D), bf16),
            pltpu.VMEM((4, 8 * PAD, HID), bf16),
            pltpu.VMEM((4, 8 * PAD, HID), bf16),
            pltpu.VMEM((4, 8, PAD, D), bf16),
            pltpu.VMEM((4, 8, PAD, D), bf16),
            pltpu.VMEM((4, PAD, D), bf16),
            pltpu.VMEM((4, PAD, D), f32),
            pltpu.VMEM((4, PAD, 128), f32),
            pltpu.VMEM((PAD, D), f32),
            pltpu.VMEM((2, PAD, D), bf16),
            pltpu.VMEM((2, 8 * PAD, HID), bf16),
            pltpu.VMEM((2, 8 * PAD, HID), bf16),
            pltpu.VMEM((D, HID), f32),
            pltpu.VMEM((HID, D), f32),
            pltpu.VMEM((D, HID), bf16),
            pltpu.VMEM((HID, D), bf16),
            dma((4,)), dma((2, NT)),
            dma((12, 9)), dma((12, 9)),
            dma((4, 8)), dma((4, 8)),
            dma((2,)), dma((2,)),
            dma((4,)), dma((4,)),
            dma((2,)), dma((2,)), dma((2,)), dma((2,)),
        ],
        compiler_params=pltpu.CompilerParams(
            collective_id=0, has_side_effects=True, vmem_limit_bytes=58 * 2**20
        ),
        cost_estimate=pl.CostEstimate(flops=11 * 10**9, bytes_accessed=13 * 10**6, transcendentals=10**6),
        name="relay_backward",
    )(*blocks)


def body(
    inputs_down, inputs_up, grads_down, grads_up, loss_grads,
    first_down, second_down, first_up, second_up, momentum_first, momentum_second,
):
    total_first, total_second, passed_down, passed_up = backward(
        inputs_down, inputs_up, grads_down, grads_up, loss_grads, first_down, second_down, first_up, second_up
    )
    new = []
    for weight, momentum, total in (
        (first_down, momentum_first, total_first), (second_down, momentum_second, total_second)
    ):
        moment = momentum_decay * momentum.astype(jnp.float32) + total[None].astype(jnp.float32)
        new.append(((weight.astype(jnp.float32) - learning_rate * moment).astype(jnp.bfloat16), moment.astype(jnp.bfloat16)))
    return (new[0][0], new[1][0], new[0][1], new[1][1], passed_down, passed_up)


def solution(mesh):
    placed = (
        P("section", None, "tensor", None),
        P("section", None, "tensor", None),
        P("section", "tensor", None),
        P("section", "tensor", None),
        P(None, "tensor", None),
        P("section", None, "tensor"),
        P("section", "tensor", None),
        P("section", None, "tensor"),
        P("section", "tensor", None),
        P("section", None, "tensor"),
        P("section", "tensor", None),
    )
    return jax.shard_map(
        body,
        mesh=mesh,
        in_specs=placed,
        out_specs=(
            P("section", None, "tensor"),
            P("section", "tensor", None),
            P("section", None, "tensor"),
            P("section", "tensor", None),
            P("section", "tensor", None),
            P("section", "tensor", None),
        ),
        check_vma=False,
    )
```

time: 250 us -> 168 us (0.67); the launches traced: 245 us -> 168 us
  Pallas kernels: 229 us -> 152 us
  local copies, waits for them, and re-layouts: 15.7 us -> 6.51 us
  other arithmetic: 0 us -> 8.5 us
    pallas_call x1, Pallas kernels: 229 us -> 152 us  [backward(): pl.pallas_call(kernel, out_shape=(jax.ShapeDtypeStruct((D, HID), bf16), j...]
    unnamed x19, local copies, waits for them, and re-layouts: 15.7 us -> 6.51 us
    convert_element_type x0 -> x2, other arithmetic: none -> 8.5 us  [body(): moment.astype(jnp.bfloat16)]
where the time goes in v2:
time: 168 us
  Pallas kernels  152 us (90%)
  other arithmetic  8.5 us (5%)
  local copies, waits for them, and re-layouts  6.51 us (4%)
    pallas_call x1, Pallas kernels, backward(): pl.pallas_call(kernel, out_shape=(jax.ShapeDtypeStruct((D, HID), bf16), j...  152 us
    convert_element_type x2, other arithmetic, body(): moment.astype(jnp.bfloat16)  8.5 us
    unnamed x19, local copies, waits for them, and re-layouts  6.51 us

profile of v2, /device:TPU:0, one launch (start us, length us, event | category | flops | bytes accessed | tf_op | source)
XLA Modules:
  0.0 167.8 jit_solution(14690375963175821202)
XLA Ops:
  0.6 1.7 %copy.17.in_down = bf16[1,2,30,2048]{3,2,1,0:T(8,128)(2,1)} copy(bf16[1,2,30,2048]{3,1,2,0:T(2,128)(2,1)} %param.11) | data formatting | bytes 491520 | tf_op args[0]
  2.4 1.7 %copy.18.in_up = bf16[1,2,30,2048]{3,2,1,0:T(8,128)(2,1)} copy(bf16[1,2,30,2048]{3,1,2,0:T(2,128)(2,1)} %param.12) | data formatting | bytes 491520 | tf_op args[1]
  4.1 1.7 %copy.19.loss = bf16[2,30,2048]{2,1,0:T(8,128)(2,1)} copy(bf16[2,30,2048]{2,0,1:T(2,128)(2,1)} %param.15) | data formatting | bytes 491520 | tf_op args[4]
  5.8 0.0 copy-start
  5.8 0.0 copy-start.1
  5.8 152.1 %relay_backward.1 = (bf16[2048,512]{1,0:T(8,128)(2,1)}, bf16[512,2048]{1,0:T(8,128)(2,1)}, bf16[1,30,2048]{2,1,0:T(8,128)(2,1)}, bf16[1,30,2048]{2,1,0:T(8,128)(2,1)}) custom-call(bf16[1,2,30,2048]{3,2,1,0:T(8,128)(2,1)} %copy.17.in_down, bf16[1,2,30,2048]{3,2,1,0:T(8,128)(2,1)} %copy.18.in_up, bf16[1,30,2048]{2,1,0:T(8,128)(2,1)} %g_down.1, ...), custom_call_target="tpu_custom_call" | custom-call | flops 11000000512 | bytes 13000000 | tf_op jit(solution)/shard_map/relay_backward/pallas_call | solution.py:401
  157.9 0.0 copy-done
  157.9 0.0 copy-done.1
  157.9 0.0 copy-start.2
  157.9 0.0 copy-start.3
  158.0 0.0 copy-start.4
  158.0 4.8 %fusion = (bf16[1,2048,512]{2,1,0:T(8,128)(2,1)}, bf16[1,2048,512]{2,1,0:T(8,128)(2,1)}) fusion(bf16[1,2048,512]{2,1,0:T(8,128)(2,1)S(1)} %copy-done, bf16[2048,512]{1,0:T(8,128)(2,1)} %get-tuple-element.10, bf16[1,2048,512]{2,1,0:T(8,128)(2,1)S(1)} %copy-done.1), kind=kLoop, calls=%fused_computation.4 | loop fusion | flops 9437184 | bytes 10485760 | tf_op jit(solution)/shard_map/convert_element_type | solution.py:457
  162.8 0.0 copy-done.2
  162.8 0.0 copy-done.3
  162.8 0.0 copy-done.4
  162.8 0.0 copy-start.6
  162.8 0.0 copy-start.5
  162.8 3.7 %fusion.1 = (bf16[1,512,2048]{2,1,0:T(8,128)(2,1)}, bf16[1,512,2048]{2,1,0:T(8,128)(2,1)}) fusion(bf16[1,512,2048]{2,1,0:T(8,128)(2,1)S(1)} %copy-done.3, bf16[512,2048]{1,0:T(8,128)(2,1)S(1)} %copy-done.4, bf16[1,512,2048]{2,1,0:T(8,128)(2,1)S(1)} %copy-done.2), kind=kLoop, calls=%fused_computation.5 | loop fusion | flops 9437184 | bytes 10485760 | tf_op jit(solution)/shard_map/convert_element_type | solution.py:457
  166.5 0.0 copy-done.6
  166.5 0.7 copy.22
  167.2 0.0 copy-done.5
  167.2 0.7 copy.23
Async XLA Ops:
  5.8 152.1 %copy-start = (bf16[1,2048,512]{2,1,0:T(8,128)(2,1)S(1)}, bf16[1,2048,512]{2,1,0:T(8,128)(2,1)}, u32[]{:S(2)}) copy-start(bf16[1,2048,512]{2,1,0:T(8,128)(2,1)} %param.20) | copy-start | bytes 6291460
  5.8 152.1 %copy-start.1 = (bf16[1,2048,512]{2,1,0:T(8,128)(2,1)S(1)}, bf16[1,2048,512]{2,1,0:T(8,128)(2,1)}, u32[]{:S(2)}) copy-start(bf16[1,2048,512]{2,1,0:T(8,128)(2,1)} %w1d_h.1) | copy-start | bytes 6291460
  157.9 4.9 %copy-start.2 = (bf16[1,512,2048]{2,1,0:T(8,128)(2,1)S(1)}, bf16[1,512,2048]{2,1,0:T(8,128)(2,1)}, u32[]{:S(2)}) copy-start(bf16[1,512,2048]{2,1,0:T(8,128)(2,1)} %w2d_h.1) | copy-start | bytes 6291460
  157.9 4.9 %copy-start.3 = (bf16[1,512,2048]{2,1,0:T(8,128)(2,1)S(1)}, bf16[1,512,2048]{2,1,0:T(8,128)(2,1)}, u32[]{:S(2)}) copy-start(bf16[1,512,2048]{2,1,0:T(8,128)(2,1)} %param.21) | copy-start | bytes 6291460
  158.0 4.9 %copy-start.4 = (bf16[512,2048]{1,0:T(8,128)(2,1)S(1)}, bf16[512,2048]{1,0:T(8,128)(2,1)}, u32[]{:S(2)}) copy-start(bf16[512,2048]{1,0:T(8,128)(2,1)} %get-tuple-element.11) | copy-start | bytes 6291460
  162.8 3.7 %copy-start.6 = (bf16[1,30,2048]{2,1,0:T(8,128)(2,1)S(1)}, bf16[1,30,2048]{2,1,0:T(8,128)(2,1)}, u32[]{:S(2)}) copy-start(bf16[1,30,2048]{2,1,0:T(8,128)(2,1)} %get-tuple-element.28) | copy-start | bytes 368644
  162.8 4.3 %copy-start.5 = (bf16[1,30,2048]{2,1,0:T(8,128)(2,1)S(1)}, bf16[1,30,2048]{2,1,0:T(8,128)(2,1)}, u32[]{:S(2)}) copy-start(bf16[1,30,2048]{2,1,0:T(8,128)(2,1)} %get-tuple-element.29) | copy-start | bytes 368644

commit v3 on v2

--- a/solution.py
+++ b/solution.py
@@ -25,13 +25,20 @@
 U1, U2, D1, D2 = range(4)
 NT = D // TILE
 HALF = PAD // 2
-MODES = (0, 0, 0, 0, 0, 1, 1, 1, 1, 0, 0, 1)
-ORDER = (
-    (0, N1D), (0, C1D), (0, N2U), (1, N1D), (1, C1D), (0, N1M), (2, N1D), (2, C1D), (1, N2U), (0, N2D), (1, N1M),
-    (2, N2U), (0, C1M), (0, C2M), (0, N2M), (1, C1M), (1, N2M), (1, N2D), (2, N1M), (2, C1M), (2, N2M), (2, N2D),
-    (1, C2M), (2, C2M),
+MODES = (1, 0, 0, 0, 0, 0, 1, 0, 0, 1, 1, 0)
+SCHEDULE = (
+    ("stage", N1U, 0), ("stage", C1U, 0), ("row", N1U), ("rest",), ("stage", C1D, 0), ("stage", N1U, 1),
+    ("stage", C1U, 1), ("stage", N1D, 0), ("stage", N1U, 2), ("stage", C1D, 1), ("stage", C1U, 2), ("row", N2U),
+    ("stage", N1D, 1), ("row", C1U), ("stage", N2D, 0), ("stage", C1D, 2), ("hidden", U1), ("stage", N1D, 2),
+    ("stage", N2M, 0), ("mirror", U1), ("pair", U1), ("hidden", D1), ("cross", U1), ("stage", N1M, 0),
+    ("pair", D1), ("finish", U1), ("stage", N2U, 0), ("cross", D1), ("relayed", 0), ("stage", C1M, 0),
+    ("stage", C2U, 0), ("finish", D1), ("row", C2U), ("stage", C1M, 1), ("stage", N2M, 1), ("relayed", 1),
+    ("stage", C2U, 1), ("stage", C2D, 0), ("stage", N2D, 1), ("stage", C2U, 2), ("stage", N2U, 1),
+    ("stage", C2M, 0), ("stage", C1M, 2), ("stage", N2D, 2), ("stage", N2U, 2), ("stage", N1M, 1),
+    ("stage", C2D, 1), ("add", 1), ("hidden", U2), ("partial", U2), ("mirror", U2), ("stage", C2D, 2),
+    ("stage", N1M, 2), ("stage", N2M, 2), ("pair", U2), ("hidden", D2), ("add", 2), ("stage", C2M, 1),
+    ("cross", U2), ("pair", D2), ("finish", U2), ("cross", D2), ("stage", C2M, 2), ("add", 3), ("finish", D2),
 )
-FILLS = (2, 1, 0, 2, 3, 2, 2, 3, 0, 3, 1, 3, 0, 1, 0, 25, 20)
 
 
 def gelu_with_slope(preact):
@@ -55,7 +62,7 @@
 def kernel(
     in_down, in_up, g_down, g_up, loss, w1d_h, w2d_h, w1u_h, w2u_h,
     t1_h, t2_h, pass_d, pass_u,
-    G, W1, W2, A, GP, PB, RR, ZB, NR, SC, CT, RL, MG, MA, ACC1, ACC2, T1, T2,
+    G, W1, W2, A, GP, PB, RR, RH, ZB, NR, SC, CT, RL, MG, MA, ACC1, ACC2, T1, T2,
     load_sem, out_sem, ag_s, ag_r, rs_s, rs_r, rl_s, rl_r, row_s, row_r, mg_s, mg_r, ma_s, ma_r,
 ):
     s = lax.axis_index("section")
@@ -73,7 +80,7 @@
     down = (lax.rem(s + 15, 16), t)
 
     barrier = pltpu.get_barrier_semaphore()
-    for peer in (xpeer(1), xpeer(2), xpeer(3), zpeer, mirror, up, down):
+    for peer in (xpeer(1), xpeer(3), zpeer, mirror, up, down):
         pl.semaphore_signal(barrier, inc=1, device_id=peer, device_id_type=MESH)
 
     loads = []
@@ -85,7 +92,7 @@
         loads.append(c)
 
     def put_normed(ref, step, q, a):
-        wide = ref[0, step].astype(jnp.float32)
+        wide = ref[...].astype(jnp.float32)[:, step]
         centred = wide - jnp.mean(wide, axis=-1, keepdims=True)
         inv = lax.rsqrt(jnp.mean(centred * centred, axis=-1, keepdims=True) + epsilon)
         NR[q, ROWS:PAD] = jnp.zeros((PAD - ROWS, D), jnp.float32)
@@ -184,25 +191,6 @@
     def row(a):
         send(G.at[a, t], G.at[N1M + a, t], row_s.at[a], row_r.at[a], mirror)
 
-    queue = list(ORDER)
-    fills = list(FILLS)
-    ready = {N1M, C1M, N2M}
-
-    def run_next():
-        k, a = queue.pop(0)
-        stage(a, k)
-
-    def fill():
-        for _ in range(fills.pop(0)):
-            if queue and (queue[0][1] < N1M or queue[0][1] in ready):
-                run_next()
-
-    def need(*arrays):
-        while any(a in arrays for _, a in queue):
-            run_next()
-        for a in arrays:
-            ag_done(a)
-
     def hidden(q, w, an, ac):
         @pl.loop(0, HID // TILE)
         def _(j):
@@ -222,30 +210,38 @@
             part = dot_nt(GP[q], W1[w, cols, :]) * D ** (-0.5)
             PB[q, :, :, cols] = part.astype(jnp.bfloat16).reshape(8, PAD, TILE)
 
+    def rs_send(q, i, src, dst, dev):
+        send(src, dst, rs_s.at[q, i], rs_r.at[q, i], dev)
+
     def rs_start(q):
-        for k in (2, 1, 3):
-            send(PB.at[q, far(k)], RR.at[q, 4 + k], rs_s.at[q, 4 + k], rs_r.at[q, 4 + k], xpeer(k))
-        for k in (2, 1, 3):
-            send(PB.at[q, near(k)], RR.at[q, k], rs_s.at[q, k], rs_r.at[q, k], xpeer(k))
+        for i, block in ((0, far(2)), (2, near(2))):
+            rs_send(q, 5 + i, PB.at[q, block, pl.ds(0, HALF)], RH.at[q, i], xpeer(1))
+            rs_send(q, 6 + i, PB.at[q, block, pl.ds(HALF, HALF)], RH.at[q, i + 1], xpeer(3))
 
     def rs_wait(q, i):
-        rcopy(RR.at[q, i], RR.at[q, i], rs_s.at[q, i], rs_r.at[q, i], zpeer).wait_recv()
+        ref = RR.at[q, i] if i < 5 else RH.at[q, i - 5]
+        rcopy(ref, ref, rs_s.at[q, i], rs_r.at[q, i], zpeer).wait_recv()
+
+    def rs_pair(q):
+        for i, place in ((0, far), (2, near)):
+            for k, half in ((1, 0), (3, 1)):
+                rs_wait(q, 5 + i + half)
+                rows = pl.ds(half * HALF, HALF)
+                both = PB[q, place(k), rows].astype(jnp.float32) + RH[q, i + half].astype(jnp.float32)
+                PB[q, place(k), rows] = both.astype(jnp.bfloat16)
+                rs_send(q, 1 + i + half, PB.at[q, place(k)], RR.at[q, 1 + i + half], xpeer(k))
 
     def rs_mid(q):
-        for k in (1, 3, 2):
-            rs_wait(q, 4 + k)
-        total = PB[q, far(0)].astype(jnp.float32)
-        for k in (1, 2, 3):
-            total = total + RR[q, 4 + k].astype(jnp.float32)
+        rs_wait(q, 1)
+        rs_wait(q, 2)
+        total = PB[q, far(0)].astype(jnp.float32) + RR[q, 1].astype(jnp.float32) + RR[q, 2].astype(jnp.float32)
         ZB[q] = total.astype(jnp.bfloat16)
-        send(ZB.at[q], RR.at[q, 0], rs_s.at[q, 0], rs_r.at[q, 0], zpeer)
+        rs_send(q, 0, ZB.at[q], RR.at[q, 0], zpeer)
 
     def rs_end(q, ac):
-        for k in (1, 3, 2):
-            rs_wait(q, k)
-        total = PB[q, t].astype(jnp.float32)
-        for k in (1, 2, 3):
-            total = total + RR[q, k].astype(jnp.float32)
+        rs_wait(q, 3)
+        rs_wait(q, 4)
+        total = PB[q, t].astype(jnp.float32) + RR[q, 3].astype(jnp.float32) + RR[q, 4].astype(jnp.float32)
         rs_wait(q, 0)
         gn = total + RR[q, 0].astype(jnp.float32)
         normed = NR[q]
@@ -262,7 +258,7 @@
 
         @pl.when(s == edge)
         def _():
-            put_rows(loss[which], a)
+            put_rows(loss[...].astype(jnp.float32)[:, which], a)
 
     def mirror_hidden(q):
         send(GP.at[q], MG.at[q], mg_s.at[q], mg_r.at[q], mirror)
@@ -300,90 +296,68 @@
                 ACC1[cols, :] = one
                 ACC2[:, cols] = two
 
+    sources = {U1: (0, N1U, C1U), U2: (0, N2U, C2U), D1: (1, N1D, C1D), D2: (1, N2D, C2D)}
+
+    def branch(q):
+        w, an, ac = sources[q]
+        for i in (2 * w, 2 * w + 1):
+            if i not in waited:
+                waited.add(i)
+                loads[i].wait()
+        ag_done(an)
+        ag_done(ac)
+        hidden(q, w, an, ac)
+        if q != U2:
+            spread(q)
+
+    def spread(q):
+        partial(q, sources[q][0])
+        rs_start(q)
+
+    def finish(q):
+        if q == U1:
+            relay(q, C1U, 0, C2U, up)
+        elif q == D1:
+            relay(q, C1D, 1, C2D, down)
+        else:
+            CT[...] = rs_end(q, sources[q][2])
+            (pass_u if q == U2 else pass_d)[0] = CT[0:ROWS].astype(jnp.bfloat16)
+
+    def relayed(i):
+        if i == 0:
+            relay_wait(0, C2U, 0, 1)
+        else:
+            relay_wait(1, C2D, 15, 0)
+
+    def rest():
+        put_normed(in_down, 0, D1, N1D)
+        put_rows(g_down[0], C1D)
+        put_normed(in_up, 1, U2, N2U)
+        put_normed(in_down, 1, D2, N2D)
+
+    def add(part):
+        if part == 1:
+            add_terms([(N1D, C1D, GP, A, D1)], first=True)
+        elif part == 2:
+            ag_done(N1M)
+            ag_done(C1M)
+            mirror_wait(U1)
+            add_terms([(N2D, C2D, GP, A, D2), (N1M, C1M, MG, MA, U1)])
+        else:
+            ag_done(N2M)
+            ag_done(C2M)
+            mirror_wait(U2)
+            add_terms([(N2M, C2M, MG, MA, U2)], last=True)
+
+    steps = dict(
+        stage=stage, row=row, rest=rest, add=add, relayed=relayed, hidden=branch, mirror=mirror_hidden,
+        partial=spread, pair=rs_pair, cross=rs_mid, finish=finish,
+    )
     put_rows(g_up[0], C1U)
     put_normed(in_up, 0, U1, N1U)
-    pl.semaphore_wait(barrier, 7)
-    row(C1U)
-    row(N1U)
-    stage(N1U, 0)
-    stage(C1U, 0)
-    put_normed(in_down, 0, D1, N1D)
-    put_rows(g_down[0], C1D)
-    put_normed(in_up, 1, U2, N2U)
-    put_normed(in_down, 1, D2, N2D)
-    row(N2U)
-    stage(N1U, 1)
-    stage(C1U, 1)
-    stage(N1U, 2)
-    stage(C1U, 2)
-    fill()
-    loads[0].wait()
-    loads[1].wait()
-    ag_done(N1U)
-    ag_done(C1U)
-    fill()
-    hidden(U1, 0, N1U, C1U)
-    partial(U1, 0)
-    rs_start(U1)
-    mirror_hidden(U1)
-    fill()
-    rs_mid(U1)
-    fill()
-    relay(U1, C1U, 0, C2U, up)
-    fill()
-    relay_wait(0, C2U, 0, 1)
-    stage(C2U, 0)
-    row(C2U)
-    ready.add(C2M)
-    fill()
-    stage(C2U, 1)
-    fill()
-    stage(C2U, 2)
-    fill()
-    need(N2U)
-    ag_done(C2U)
-    hidden(U2, 0, N2U, C2U)
-    mirror_hidden(U2)
-    need(N1D, C1D)
-    loads[2].wait()
-    loads[3].wait()
-    hidden(D1, 1, N1D, C1D)
-    partial(D1, 1)
-    rs_start(D1)
-    fill()
-    partial(U2, 0)
-    add_terms([(N1D, C1D, GP, A, D1)], first=True)
-    rs_mid(D1)
-    fill()
-    relay(D1, C1D, 1, C2D, down)
-    fill()
-    relay_wait(1, C2D, 15, 0)
-    stage(C2D, 0)
-    fill()
-    stage(C2D, 1)
-    fill()
-    rs_start(U2)
-    stage(C2D, 2)
-    fill()
-    need(N2D)
-    ag_done(C2D)
-    hidden(D2, 1, N2D, C2D)
-    partial(D2, 1)
-    rs_start(D2)
-    fill()
-    rs_mid(U2)
-    fill()
-    need(N1M, C1M)
-    mirror_wait(U1)
-    add_terms([(N2D, C2D, GP, A, D2), (N1M, C1M, MG, MA, U1)])
-    CT[...] = rs_end(U2, C2U)
-    pass_u[0] = CT[0:ROWS].astype(jnp.bfloat16)
-    rs_mid(D2)
-    need(N2M, C2M)
-    mirror_wait(U2)
-    add_terms([(N2M, C2M, MG, MA, U2)], last=True)
-    CT[...] = rs_end(D2, C2D)
-    pass_d[0] = CT[0:ROWS].astype(jnp.bfloat16)
+    pl.semaphore_wait(barrier, 6)
+    for step, *where in SCHEDULE:
+        steps[step](*where)
     for c in pending:
         c.wait_send()
 
@@ -415,7 +389,8 @@
             pltpu.VMEM((4, 8 * PAD, HID), bf16),
             pltpu.VMEM((4, 8 * PAD, HID), bf16),
             pltpu.VMEM((4, 8, PAD, D), bf16),
-            pltpu.VMEM((4, 8, PAD, D), bf16),
+            pltpu.VMEM((4, 5, PAD, D), bf16),
+            pltpu.VMEM((4, 4, HALF, D), bf16),
             pltpu.VMEM((4, PAD, D), bf16),
             pltpu.VMEM((4, PAD, D), f32),
             pltpu.VMEM((4, PAD, 128), f32),
@@ -429,7 +404,7 @@
             pltpu.VMEM((HID, D), bf16),
             dma((4,)), dma((2, NT)),
             dma((12, 9)), dma((12, 9)),
-            dma((4, 8)), dma((4, 8)),
+            dma((4, 9)), dma((4, 9)),
             dma((2,)), dma((2,)),
             dma((4,)), dma((4,)),
             dma((2,)), dma((2,)), dma((2,)), dma((2,)),
@@ -447,7 +422,8 @@
     first_down, second_down, first_up, second_up, momentum_first, momentum_second,
 ):
     total_first, total_second, passed_down, passed_up = backward(
-        inputs_down, inputs_up, grads_down, grads_up, loss_grads, first_down, second_down, first_up, second_up
+        jnp.swapaxes(inputs_down[0], 0, 1), jnp.swapaxes(inputs_up[0], 0, 1), grads_down, grads_up,
+        jnp.swapaxes(loss_grads, 0, 1), first_down, second_down, first_up, second_up,
     )
     new = []
     for weight, momentum, total in (

time: 168 us -> 159 us (0.946)
  local copies, waits for them, and re-layouts: 6.51 us -> 1.34 us
  Pallas kernels: 152 us -> 148 us
    unnamed x19 -> x16, local copies, waits for them, and re-layouts: 6.51 us -> 1.34 us
    pallas_call x1, Pallas kernels: 152 us -> 148 us  [backward(): pl.pallas_call(kernel, out_shape=(jax.ShapeDtypeStruct((D, HID), bf16), j...]
where the time goes in v3:
time: 159 us
  Pallas kernels  148 us (93%)
  other arithmetic  8.5 us (5%)
    pallas_call x1, Pallas kernels, backward(): pl.pallas_call(kernel, out_shape=(jax.ShapeDtypeStruct((D, HID), bf16), j...  148 us
    convert_element_type x2, other arithmetic, body(): moment.astype(jnp.bfloat16)  8.5 us

profile of v3, /device:TPU:0, one launch (start us, length us, event | category | flops | bytes accessed | tf_op | source)
XLA Modules:
  0.0 158.7 jit_solution(7565955909510623831)
XLA Ops:
  0.6 0.0 copy-start
  0.6 0.0 copy-start.1
  0.7 148.2 %relay_backward.1 = (bf16[2048,512]{1,0:T(8,128)(2,1)}, bf16[512,2048]{1,0:T(8,128)(2,1)}, bf16[1,30,2048]{2,1,0:T(8,128)(2,1)}, bf16[1,30,2048]{2,1,0:T(8,128)(2,1)}) custom-call(bf16[30,2,2048]{2,1,0:T(2,128)(2,1)} %bitcast.15, bf16[30,2,2048]{2,1,0:T(2,128)(2,1)} %bitcast.16, bf16[1,30,2048]{2,1,0:T(8,128)(2,1)} %g_down.1, bf16[1,30,2048]{2,1,0:T(8,128)(2,1)} %g_up.1, ...), custom_call_target="tpu_custom_call" | custom-call | flops 11000000512 | bytes 13000000 | tf_op jit(solution)/shard_map/relay_backward/pallas_call | solution.py:375
  148.8 0.0 copy-done
  148.8 0.0 copy-done.1
  148.8 0.0 copy-start.2
  148.9 0.0 copy-start.3
  148.9 0.0 copy-start.4
  148.9 4.8 %fusion = (bf16[1,2048,512]{2,1,0:T(8,128)(2,1)}, bf16[1,2048,512]{2,1,0:T(8,128)(2,1)}) fusion(bf16[1,2048,512]{2,1,0:T(8,128)(2,1)S(1)} %copy-done, bf16[2048,512]{1,0:T(8,128)(2,1)} %get-tuple-element.10, bf16[1,2048,512]{2,1,0:T(8,128)(2,1)S(1)} %copy-done.1), kind=kLoop, calls=%fused_computation.4 | loop fusion | flops 9437184 | bytes 10485760 | tf_op jit(solution)/shard_map/convert_element_type | solution.py:433
  153.7 0.0 copy-done.2
  153.7 0.0 copy-done.3
  153.7 0.0 copy-done.4
  153.7 0.0 copy-start.6
  153.7 0.0 copy-start.5
  153.8 3.7 %fusion.1 = (bf16[1,512,2048]{2,1,0:T(8,128)(2,1)}, bf16[1,512,2048]{2,1,0:T(8,128)(2,1)}) fusion(bf16[1,512,2048]{2,1,0:T(8,128)(2,1)S(1)} %copy-done.3, bf16[512,2048]{1,0:T(8,128)(2,1)S(1)} %copy-done.4, bf16[1,512,2048]{2,1,0:T(8,128)(2,1)S(1)} %copy-done.2), kind=kLoop, calls=%fused_computation.5 | loop fusion | flops 9437184 | bytes 10485760 | tf_op jit(solution)/shard_map/convert_element_type | solution.py:433
  157.4 0.0 copy-done.6
  157.4 0.7 copy.19
  158.1 0.0 copy-done.5
  158.1 0.7 copy.20
Async XLA Ops:
  0.6 148.2 %copy-start = (bf16[1,2048,512]{2,1,0:T(8,128)(2,1)S(1)}, bf16[1,2048,512]{2,1,0:T(8,128)(2,1)}, u32[]{:S(2)}) copy-start(bf16[1,2048,512]{2,1,0:T(8,128)(2,1)} %param.20) | copy-start | bytes 6291460
  0.6 148.2 %copy-start.1 = (bf16[1,2048,512]{2,1,0:T(8,128)(2,1)S(1)}, bf16[1,2048,512]{2,1,0:T(8,128)(2,1)}, u32[]{:S(2)}) copy-start(bf16[1,2048,512]{2,1,0:T(8,128)(2,1)} %w1d_h.1) | copy-start | bytes 6291460
  148.8 4.9 %copy-start.2 = (bf16[1,512,2048]{2,1,0:T(8,128)(2,1)S(1)}, bf16[1,512,2048]{2,1,0:T(8,128)(2,1)}, u32[]{:S(2)}) copy-start(bf16[1,512,2048]{2,1,0:T(8,128)(2,1)} %w2d_h.1) | copy-start | bytes 6291460
  148.9 4.9 %copy-start.3 = (bf16[1,512,2048]{2,1,0:T(8,128)(2,1)S(1)}, bf16[1,512,2048]{2,1,0:T(8,128)(2,1)}, u32[]{:S(2)}) copy-start(bf16[1,512,2048]{2,1,0:T(8,128)(2,1)} %param.21) | copy-start | bytes 6291460
  148.9 4.9 %copy-start.4 = (bf16[512,2048]{1,0:T(8,128)(2,1)S(1)}, bf16[512,2048]{1,0:T(8,128)(2,1)}, u32[]{:S(2)}) copy-start(bf16[512,2048]{1,0:T(8,128)(2,1)} %get-tuple-element.11) | copy-start | bytes 6291460
  153.7 3.7 %copy-start.6 = (bf16[1,30,2048]{2,1,0:T(8,128)(2,1)S(1)}, bf16[1,30,2048]{2,1,0:T(8,128)(2,1)}, u32[]{:S(2)}) copy-start(bf16[1,30,2048]{2,1,0:T(8,128)(2,1)} %get-tuple-element.28) | copy-start | bytes 368644
  153.7 4.3 %copy-start.5 = (bf16[1,30,2048]{2,1,0:T(8,128)(2,1)S(1)}, bf16[1,30,2048]{2,1,0:T(8,128)(2,1)}, u32[]{:S(2)}) copy-start(bf16[1,30,2048]{2,1,0:T(8,128)(2,1)} %get-tuple-element.29) | copy-start | bytes 368644

commit v4 on v3

--- a/solution.py
+++ b/solution.py
@@ -25,19 +25,20 @@
 U1, U2, D1, D2 = range(4)
 NT = D // TILE
 HALF = PAD // 2
-MODES = (1, 0, 0, 0, 0, 0, 1, 0, 0, 1, 1, 0)
+MODES = (1, 0, 1, 0, 0, 1, 0, 0, 0, 1, 1, 0)
 SCHEDULE = (
-    ("stage", N1U, 0), ("stage", C1U, 0), ("row", N1U), ("rest",), ("stage", C1D, 0), ("stage", N1U, 1),
-    ("stage", C1U, 1), ("stage", N1D, 0), ("stage", N1U, 2), ("stage", C1D, 1), ("stage", C1U, 2), ("row", N2U),
-    ("stage", N1D, 1), ("row", C1U), ("stage", N2D, 0), ("stage", C1D, 2), ("hidden", U1), ("stage", N1D, 2),
-    ("stage", N2M, 0), ("mirror", U1), ("pair", U1), ("hidden", D1), ("cross", U1), ("stage", N1M, 0),
-    ("pair", D1), ("finish", U1), ("stage", N2U, 0), ("cross", D1), ("relayed", 0), ("stage", C1M, 0),
-    ("stage", C2U, 0), ("finish", D1), ("row", C2U), ("stage", C1M, 1), ("stage", N2M, 1), ("relayed", 1),
-    ("stage", C2U, 1), ("stage", C2D, 0), ("stage", N2D, 1), ("stage", C2U, 2), ("stage", N2U, 1),
-    ("stage", C2M, 0), ("stage", C1M, 2), ("stage", N2D, 2), ("stage", N2U, 2), ("stage", N1M, 1),
-    ("stage", C2D, 1), ("add", 1), ("hidden", U2), ("partial", U2), ("mirror", U2), ("stage", C2D, 2),
-    ("stage", N1M, 2), ("stage", N2M, 2), ("pair", U2), ("hidden", D2), ("add", 2), ("stage", C2M, 1),
-    ("cross", U2), ("pair", D2), ("finish", U2), ("cross", D2), ("stage", C2M, 2), ("add", 3), ("finish", D2),
+    ("stage", C1U, 0), ("row", C1U), ("stage", N1U, 0), ("rest",), ("row", N1U), ("stage", N1D, 0),
+    ("stage", N1U, 1), ("stage", C1U, 1), ("stage", N1U, 2), ("stage", C1D, 0), ("stage", C1U, 2),
+    ("stage", N2D, 0), ("stage", C1D, 1), ("stage", N1D, 1), ("stage", C1M, 0), ("hidden", U1),
+    ("stage", C1D, 2), ("stage", N1D, 2), ("pair", U1), ("stage", N1M, 0), ("stage", N2U, 0), ("cross", U1),
+    ("row", N2U), ("stage", C1M, 1), ("hidden", D1), ("stage", N1M, 1), ("finish", U1), ("pair", D1),
+    ("stage", N2U, 1), ("add", 1), ("relayed", 0), ("stage", C2U, 0), ("cross", D1), ("row", C2U),
+    ("stage", N2M, 0), ("stage", N2D, 1), ("stage", C2U, 1), ("stage", N2U, 2), ("finish", D1),
+    ("stage", C2M, 0), ("relayed", 1), ("stage", C2D, 0), ("mirror", U1), ("stage", C2U, 2), ("stage", C2M, 1),
+    ("stage", C2D, 1), ("stage", N2D, 2), ("stage", C1M, 2), ("hidden", U2), ("partial", U2), ("mirror", U2),
+    ("stage", C2D, 2), ("stage", N1M, 2), ("pair", U2), ("stage", N2M, 1), ("hidden", D2), ("stage", C2M, 2),
+    ("add", 2), ("cross", U2), ("stage", N2M, 2), ("pair", D2), ("cross", D2), ("finish", U2), ("add", 3),
+    ("finish", D2),
 )
 
 

time: 159 us -> 152 us (0.956)
  Pallas kernels: 148 us -> 141 us
    pallas_call x1, Pallas kernels: 148 us -> 141 us  [backward(): pl.pallas_call(kernel, out_shape=(jax.ShapeDtypeStruct((D, HID), bf16), j...]
where the time goes in v4:
time: 152 us
  Pallas kernels  141 us (93%)
  other arithmetic  8.5 us (6%)
    pallas_call x1, Pallas kernels, backward(): pl.pallas_call(kernel, out_shape=(jax.ShapeDtypeStruct((D, HID), bf16), j...  141 us
    convert_element_type x2, other arithmetic, body(): moment.astype(jnp.bfloat16)  8.5 us

profile of v4, /device:TPU:0, one launch (start us, length us, event | category | flops | bytes accessed | tf_op | source)
XLA Modules:
  0.0 151.9 jit_solution(10918452331896593621)
XLA Ops:
  0.6 0.0 copy-start
  0.6 0.0 copy-start.1
  0.7 141.4 %relay_backward.1 = (bf16[2048,512]{1,0:T(8,128)(2,1)}, bf16[512,2048]{1,0:T(8,128)(2,1)}, bf16[1,30,2048]{2,1,0:T(8,128)(2,1)}, bf16[1,30,2048]{2,1,0:T(8,128)(2,1)}) custom-call(bf16[30,2,2048]{2,1,0:T(2,128)(2,1)} %bitcast.15, bf16[30,2,2048]{2,1,0:T(2,128)(2,1)} %bitcast.16, bf16[1,30,2048]{2,1,0:T(8,128)(2,1)} %g_down.1, bf16[1,30,2048]{2,1,0:T(8,128)(2,1)} %g_up.1, ...), custom_call_target="tpu_custom_call" | custom-call | flops 11000000512 | bytes 13000000 | tf_op jit(solution)/shard_map/relay_backward/pallas_call | solution.py:376
  142.0 0.0 copy-done
  142.0 0.0 copy-done.1
  142.0 0.0 copy-start.2
  142.1 0.0 copy-start.3
  142.1 0.0 copy-start.4
  142.1 4.8 %fusion = (bf16[1,2048,512]{2,1,0:T(8,128)(2,1)}, bf16[1,2048,512]{2,1,0:T(8,128)(2,1)}) fusion(bf16[1,2048,512]{2,1,0:T(8,128)(2,1)S(1)} %copy-done, bf16[2048,512]{1,0:T(8,128)(2,1)} %get-tuple-element.10, bf16[1,2048,512]{2,1,0:T(8,128)(2,1)S(1)} %copy-done.1), kind=kLoop, calls=%fused_computation.4 | loop fusion | flops 9437184 | bytes 10485760 | tf_op jit(solution)/shard_map/convert_element_type | solution.py:434
  146.9 0.0 copy-done.2
  146.9 0.0 copy-done.3
  146.9 0.0 copy-done.4
  146.9 0.0 copy-start.6
  146.9 0.0 copy-start.5
  146.9 3.7 %fusion.1 = (bf16[1,512,2048]{2,1,0:T(8,128)(2,1)}, bf16[1,512,2048]{2,1,0:T(8,128)(2,1)}) fusion(bf16[1,512,2048]{2,1,0:T(8,128)(2,1)S(1)} %copy-done.3, bf16[512,2048]{1,0:T(8,128)(2,1)S(1)} %copy-done.4, bf16[1,512,2048]{2,1,0:T(8,128)(2,1)S(1)} %copy-done.2), kind=kLoop, calls=%fused_computation.5 | loop fusion | flops 9437184 | bytes 10485760 | tf_op jit(solution)/shard_map/convert_element_type | solution.py:434
  150.6 0.0 copy-done.6
  150.6 0.7 copy.19
  151.3 0.0 copy-done.5
  151.3 0.7 copy.20
Async XLA Ops:
  0.6 141.4 %copy-start = (bf16[1,2048,512]{2,1,0:T(8,128)(2,1)S(1)}, bf16[1,2048,512]{2,1,0:T(8,128)(2,1)}, u32[]{:S(2)}) copy-start(bf16[1,2048,512]{2,1,0:T(8,128)(2,1)} %param.20) | copy-start | bytes 6291460
  0.6 141.4 %copy-start.1 = (bf16[1,2048,512]{2,1,0:T(8,128)(2,1)S(1)}, bf16[1,2048,512]{2,1,0:T(8,128)(2,1)}, u32[]{:S(2)}) copy-start(bf16[1,2048,512]{2,1,0:T(8,128)(2,1)} %w1d_h.1) | copy-start | bytes 6291460
  142.0 4.9 %copy-start.2 = (bf16[1,512,2048]{2,1,0:T(8,128)(2,1)S(1)}, bf16[1,512,2048]{2,1,0:T(8,128)(2,1)}, u32[]{:S(2)}) copy-start(bf16[1,512,2048]{2,1,0:T(8,128)(2,1)} %w2d_h.1) | copy-start | bytes 6291460
  142.1 4.9 %copy-start.3 = (bf16[1,512,2048]{2,1,0:T(8,128)(2,1)S(1)}, bf16[1,512,2048]{2,1,0:T(8,128)(2,1)}, u32[]{:S(2)}) copy-start(bf16[1,512,2048]{2,1,0:T(8,128)(2,1)} %param.21) | copy-start | bytes 6291460
  142.1 4.9 %copy-start.4 = (bf16[512,2048]{1,0:T(8,128)(2,1)S(1)}, bf16[512,2048]{1,0:T(8,128)(2,1)}, u32[]{:S(2)}) copy-start(bf16[512,2048]{1,0:T(8,128)(2,1)} %get-tuple-element.11) | copy-start | bytes 6291460
  146.9 3.7 %copy-start.6 = (bf16[1,30,2048]{2,1,0:T(8,128)(2,1)S(1)}, bf16[1,30,2048]{2,1,0:T(8,128)(2,1)}, u32[]{:S(2)}) copy-start(bf16[1,30,2048]{2,1,0:T(8,128)(2,1)} %get-tuple-element.28) | copy-start | bytes 368644
  146.9 4.3 %copy-start.5 = (bf16[1,30,2048]{2,1,0:T(8,128)(2,1)S(1)}, bf16[1,30,2048]{2,1,0:T(8,128)(2,1)}, u32[]{:S(2)}) copy-start(bf16[1,30,2048]{2,1,0:T(8,128)(2,1)} %get-tuple-element.29) | copy-start | bytes 368644

commit v5 on v4

--- a/solution.py
+++ b/solution.py
@@ -25,7 +25,7 @@
 U1, U2, D1, D2 = range(4)
 NT = D // TILE
 HALF = PAD // 2
-MODES = (1, 0, 1, 0, 0, 1, 0, 0, 0, 1, 1, 0)
+MODES = (1, 0, 0, 0, 0, 1, 0, 0, 0, 1, 1, 0)
 SCHEDULE = (
     ("stage", C1U, 0), ("row", C1U), ("stage", N1U, 0), ("rest",), ("row", N1U), ("stage", N1D, 0),
     ("stage", N1U, 1), ("stage", C1U, 1), ("stage", N1U, 2), ("stage", C1D, 0), ("stage", C1U, 2),

time: 152 us -> 147 us (0.967)
  Pallas kernels: 141 us -> 136 us
    pallas_call x1, Pallas kernels: 141 us -> 136 us  [backward(): pl.pallas_call(kernel, out_shape=(jax.ShapeDtypeStruct((D, HID), bf16), j...]
where the time goes in v5:
time: 147 us
  Pallas kernels  136 us (93%)
  other arithmetic  8.5 us (6%)
    pallas_call x1, Pallas kernels, backward(): pl.pallas_call(kernel, out_shape=(jax.ShapeDtypeStruct((D, HID), bf16), j...  136 us
    convert_element_type x2, other arithmetic, body(): moment.astype(jnp.bfloat16)  8.5 us

profile of v5, /device:TPU:0, one launch (start us, length us, event | category | flops | bytes accessed | tf_op | source)
XLA Modules:
  0.0 146.9 jit_solution(2366040239850587008)
XLA Ops:
  0.6 0.0 copy-start
  0.6 0.0 copy-start.1
  0.7 136.3 %relay_backward.1 = (bf16[2048,512]{1,0:T(8,128)(2,1)}, bf16[512,2048]{1,0:T(8,128)(2,1)}, bf16[1,30,2048]{2,1,0:T(8,128)(2,1)}, bf16[1,30,2048]{2,1,0:T(8,128)(2,1)}) custom-call(bf16[30,2,2048]{2,1,0:T(2,128)(2,1)} %bitcast.15, bf16[30,2,2048]{2,1,0:T(2,128)(2,1)} %bitcast.16, bf16[1,30,2048]{2,1,0:T(8,128)(2,1)} %g_down.1, bf16[1,30,2048]{2,1,0:T(8,128)(2,1)} %g_up.1, ...), custom_call_target="tpu_custom_call" | custom-call | flops 11000000512 | bytes 13000000 | tf_op jit(solution)/shard_map/relay_backward/pallas_call | solution.py:376
  136.9 0.0 copy-done
  137.0 0.0 copy-done.1
  137.0 0.0 copy-start.2
  137.0 0.0 copy-start.3
  137.0 0.0 copy-start.4
  137.0 4.8 %fusion = (bf16[1,2048,512]{2,1,0:T(8,128)(2,1)}, bf16[1,2048,512]{2,1,0:T(8,128)(2,1)}) fusion(bf16[1,2048,512]{2,1,0:T(8,128)(2,1)S(1)} %copy-done, bf16[2048,512]{1,0:T(8,128)(2,1)} %get-tuple-element.10, bf16[1,2048,512]{2,1,0:T(8,128)(2,1)S(1)} %copy-done.1), kind=kLoop, calls=%fused_computation.4 | loop fusion | flops 9437184 | bytes 10485760 | tf_op jit(solution)/shard_map/convert_element_type | solution.py:434
  141.8 0.0 copy-done.2
  141.8 0.0 copy-done.3
  141.8 0.0 copy-done.4
  141.9 0.0 copy-start.6
  141.9 0.0 copy-start.5
  141.9 3.7 %fusion.1 = (bf16[1,512,2048]{2,1,0:T(8,128)(2,1)}, bf16[1,512,2048]{2,1,0:T(8,128)(2,1)}) fusion(bf16[1,512,2048]{2,1,0:T(8,128)(2,1)S(1)} %copy-done.3, bf16[512,2048]{1,0:T(8,128)(2,1)S(1)} %copy-done.4, bf16[1,512,2048]{2,1,0:T(8,128)(2,1)S(1)} %copy-done.2), kind=kLoop, calls=%fused_computation.5 | loop fusion | flops 9437184 | bytes 10485760 | tf_op jit(solution)/shard_map/convert_element_type | solution.py:434
  145.5 0.0 copy-done.6
  145.5 0.7 copy.19
  146.2 0.0 copy-done.5
  146.2 0.7 copy.20
Async XLA Ops:
  0.6 136.3 %copy-start = (bf16[1,2048,512]{2,1,0:T(8,128)(2,1)S(1)}, bf16[1,2048,512]{2,1,0:T(8,128)(2,1)}, u32[]{:S(2)}) copy-start(bf16[1,2048,512]{2,1,0:T(8,128)(2,1)} %param.20) | copy-start | bytes 6291460
  0.6 136.3 %copy-start.1 = (bf16[1,2048,512]{2,1,0:T(8,128)(2,1)S(1)}, bf16[1,2048,512]{2,1,0:T(8,128)(2,1)}, u32[]{:S(2)}) copy-start(bf16[1,2048,512]{2,1,0:T(8,128)(2,1)} %w1d_h.1) | copy-start | bytes 6291460
  137.0 4.9 %copy-start.2 = (bf16[1,512,2048]{2,1,0:T(8,128)(2,1)S(1)}, bf16[1,512,2048]{2,1,0:T(8,128)(2,1)}, u32[]{:S(2)}) copy-start(bf16[1,512,2048]{2,1,0:T(8,128)(2,1)} %w2d_h.1) | copy-start | bytes 6291460
  137.0 4.9 %copy-start.3 = (bf16[1,512,2048]{2,1,0:T(8,128)(2,1)S(1)}, bf16[1,512,2048]{2,1,0:T(8,128)(2,1)}, u32[]{:S(2)}) copy-start(bf16[1,512,2048]{2,1,0:T(8,128)(2,1)} %param.21) | copy-start | bytes 6291460
  137.0 4.9 %copy-start.4 = (bf16[512,2048]{1,0:T(8,128)(2,1)S(1)}, bf16[512,2048]{1,0:T(8,128)(2,1)}, u32[]{:S(2)}) copy-start(bf16[512,2048]{1,0:T(8,128)(2,1)} %get-tuple-element.11) | copy-start | bytes 6291460
  141.9 3.7 %copy-start.6 = (bf16[1,30,2048]{2,1,0:T(8,128)(2,1)S(1)}, bf16[1,30,2048]{2,1,0:T(8,128)(2,1)}, u32[]{:S(2)}) copy-start(bf16[1,30,2048]{2,1,0:T(8,128)(2,1)} %get-tuple-element.28) | copy-start | bytes 368644
  141.9 4.3 %copy-start.5 = (bf16[1,30,2048]{2,1,0:T(8,128)(2,1)S(1)}, bf16[1,30,2048]{2,1,0:T(8,128)(2,1)}, u32[]{:S(2)}) copy-start(bf16[1,30,2048]{2,1,0:T(8,128)(2,1)} %get-tuple-element.29) | copy-start | bytes 368644

commit v6 on v5

--- a/solution.py
+++ b/solution.py
@@ -25,7 +25,7 @@
 U1, U2, D1, D2 = range(4)
 NT = D // TILE
 HALF = PAD // 2
-MODES = (1, 0, 0, 0, 0, 1, 0, 0, 0, 1, 1, 0)
+MODES = (1, 0, 0, 0, 0, 1, 0, 0, 0, 0, 1, 0)
 SCHEDULE = (
     ("stage", C1U, 0), ("row", C1U), ("stage", N1U, 0), ("rest",), ("row", N1U), ("stage", N1D, 0),
     ("stage", N1U, 1), ("stage", C1U, 1), ("stage", N1U, 2), ("stage", C1D, 0), ("stage", C1U, 2),

time: 147 us -> 152 us (1.034)
  Pallas kernels: 136 us -> 141 us
    pallas_call x1, Pallas kernels: 136 us -> 141 us  [backward(): pl.pallas_call(kernel, out_shape=(jax.ShapeDtypeStruct((D, HID), bf16), j...]
where the time goes in v6:
time: 152 us; the launch traced here: 151 us
  Pallas kernels  141 us (93%)
  other arithmetic  8.5 us (6%)
    pallas_call x1, Pallas kernels, backward(): pl.pallas_call(kernel, out_shape=(jax.ShapeDtypeStruct((D, HID), bf16), j...  141 us
    convert_element_type x2, other arithmetic, body(): moment.astype(jnp.bfloat16)  8.5 us

profile of v6, /device:TPU:0, one launch (start us, length us, event | category | flops | bytes accessed | tf_op | source)
XLA Modules:
  0.0 151.1 jit_solution(10050201254916179214)
XLA Ops:
  0.6 0.0 copy-start
  0.6 0.0 copy-start.1
  0.7 140.5 %relay_backward.1 = (bf16[2048,512]{1,0:T(8,128)(2,1)}, bf16[512,2048]{1,0:T(8,128)(2,1)}, bf16[1,30,2048]{2,1,0:T(8,128)(2,1)}, bf16[1,30,2048]{2,1,0:T(8,128)(2,1)}) custom-call(bf16[30,2,2048]{2,1,0:T(2,128)(2,1)} %bitcast.15, bf16[30,2,2048]{2,1,0:T(2,128)(2,1)} %bitcast.16, bf16[1,30,2048]{2,1,0:T(8,128)(2,1)} %g_down.1, bf16[1,30,2048]{2,1,0:T(8,128)(2,1)} %g_up.1, ...), custom_call_target="tpu_custom_call" | custom-call | flops 11000000512 | bytes 13000000 | tf_op jit(solution)/shard_map/relay_backward/pallas_call | solution.py:376
  141.2 0.0 copy-done
  141.2 0.0 copy-done.1
  141.2 0.0 copy-start.2
  141.2 0.0 copy-start.3
  141.2 0.0 copy-start.4
  141.2 4.8 %fusion = (bf16[1,2048,512]{2,1,0:T(8,128)(2,1)}, bf16[1,2048,512]{2,1,0:T(8,128)(2,1)}) fusion(bf16[1,2048,512]{2,1,0:T(8,128)(2,1)S(1)} %copy-done, bf16[2048,512]{1,0:T(8,128)(2,1)} %get-tuple-element.10, bf16[1,2048,512]{2,1,0:T(8,128)(2,1)S(1)} %copy-done.1), kind=kLoop, calls=%fused_computation.4 | loop fusion | flops 9437184 | bytes 10485760 | tf_op jit(solution)/shard_map/convert_element_type | solution.py:434
  146.1 0.0 copy-done.2
  146.1 0.0 copy-done.3
  146.1 0.0 copy-done.4
  146.1 0.0 copy-start.6
  146.1 0.0 copy-start.5
  146.1 3.7 %fusion.1 = (bf16[1,512,2048]{2,1,0:T(8,128)(2,1)}, bf16[1,512,2048]{2,1,0:T(8,128)(2,1)}) fusion(bf16[1,512,2048]{2,1,0:T(8,128)(2,1)S(1)} %copy-done.3, bf16[512,2048]{1,0:T(8,128)(2,1)S(1)} %copy-done.4, bf16[1,512,2048]{2,1,0:T(8,128)(2,1)S(1)} %copy-done.2), kind=kLoop, calls=%fused_computation.5 | loop fusion | flops 9437184 | bytes 10485760 | tf_op jit(solution)/shard_map/convert_element_type | solution.py:434
  149.8 0.0 copy-done.6
  149.8 0.7 copy.19
  150.4 0.0 copy-done.5
  150.4 0.7 copy.20
Async XLA Ops:
  0.6 140.5 %copy-start = (bf16[1,2048,512]{2,1,0:T(8,128)(2,1)S(1)}, bf16[1,2048,512]{2,1,0:T(8,128)(2,1)}, u32[]{:S(2)}) copy-start(bf16[1,2048,512]{2,1,0:T(8,128)(2,1)} %param.20) | copy-start | bytes 6291460
  0.6 140.5 %copy-start.1 = (bf16[1,2048,512]{2,1,0:T(8,128)(2,1)S(1)}, bf16[1,2048,512]{2,1,0:T(8,128)(2,1)}, u32[]{:S(2)}) copy-start(bf16[1,2048,512]{2,1,0:T(8,128)(2,1)} %w1d_h.1) | copy-start | bytes 6291460
  141.2 4.9 %copy-start.2 = (bf16[1,512,2048]{2,1,0:T(8,128)(2,1)S(1)}, bf16[1,512,2048]{2,1,0:T(8,128)(2,1)}, u32[]{:S(2)}) copy-start(bf16[1,512,2048]{2,1,0:T(8,128)(2,1)} %w2d_h.1) | copy-start | bytes 6291460
  141.2 4.9 %copy-start.3 = (bf16[1,512,2048]{2,1,0:T(8,128)(2,1)S(1)}, bf16[1,512,2048]{2,1,0:T(8,128)(2,1)}, u32[]{:S(2)}) copy-start(bf16[1,512,2048]{2,1,0:T(8,128)(2,1)} %param.21) | copy-start | bytes 6291460
  141.2 4.9 %copy-start.4 = (bf16[512,2048]{1,0:T(8,128)(2,1)S(1)}, bf16[512,2048]{1,0:T(8,128)(2,1)}, u32[]{:S(2)}) copy-start(bf16[512,2048]{1,0:T(8,128)(2,1)} %get-tuple-element.11) | copy-start | bytes 6291460
  146.1 3.7 %copy-start.6 = (bf16[1,30,2048]{2,1,0:T(8,128)(2,1)S(1)}, bf16[1,30,2048]{2,1,0:T(8,128)(2,1)}, u32[]{:S(2)}) copy-start(bf16[1,30,2048]{2,1,0:T(8,128)(2,1)} %get-tuple-element.28) | copy-start | bytes 368644
  146.1 4.3 %copy-start.5 = (bf16[1,30,2048]{2,1,0:T(8,128)(2,1)S(1)}, bf16[1,30,2048]{2,1,0:T(8,128)(2,1)}, u32[]{:S(2)}) copy-start(bf16[1,30,2048]{2,1,0:T(8,128)(2,1)} %get-tuple-element.29) | copy-start | bytes 368644
